TPU v7x, 256 devices: a whole 4x4x8 slice. The times are simulated.
256 devices in a mesh: py: 16 (over z_hi, y), pz: 16 (over x, z_lo, core).
Axes of the slice: x: 4, y: 4, z: 8 (z_hi: 4, z_lo: 2; z = z_hi * 2 + z_lo), core: 2. Of those that a mesh axis runs over, the one named last changes fastest.
Arguments:
- solid: int32 [256, 512, 512], P('py', 'pz'), may hold values 0 or 1
- orientation: float32 [256, 512, 512], P('py', 'pz'), may hold values from -6 to 6
Outputs:
- power_solid: float32 [512, 512, 256], P('py', 'pz')
- power_orient: float32 [512, 512, 256], P('py', 'pz')
- cross: float32 [2, 512, 512, 256], P(None, 'py', 'pz')
Inputs may be any that keep to these rules, and one draw needn't show every extreme that they name: 0 marks pore space, 1 marks solid.
All inputs are finite; a program needn't handle non-finite values. No bound on the sum of `solid` on one device may be relied on, other than what follows from the above.
Results may differ from a plain program's by a relative error of at most 0.0003.
Values sent between devices are 32-bit elements; how exact they have to be, the bound alone decides.
No kernel may reach another device: no remote copies, remote signals or barrier semaphores. Data moves between devices by JAX's collectives and lax.ppermute only.
A program may use at most 128 MiB of HBM per device.

v0:
```python
import math

import jax
import jax.numpy as jnp
from jax import lax
from jax.sharding import PartitionSpec as P


def from_partner(shard, axis, apart):
    return lax.ppermute(shard, axis, [(i, i ^ 1 << apart) for i in range(lax.axis_size(axis))])


def from_behind(shard, axis, by):
    devices = lax.axis_size(axis)
    return lax.ppermute(shard, axis, [(i, (i + by) % devices) for i in range(devices)])


def table(length):
    counter = jnp.arange(length, dtype=jnp.int32)
    products = counter[:, None] * counter[None, :] % length
    angles = products.astype(jnp.float32) * (2.0 * math.pi / length)
    return jnp.concatenate([jnp.cos(angles), -jnp.sin(angles)], 1)


def transform(real_part, imag_part, form, length):
    joined = table(length)
    first = jnp.einsum(form, real_part, joined, precision=lax.Precision.HIGHEST)
    second = jnp.einsum(form, imag_part, joined, precision=lax.Precision.HIGHEST)
    new_real = first[..., :length] - second[..., length:]
    new_imag = second[..., :length] + first[..., length:]
    return (new_real, new_imag)


def reflect(values, dimension):
    return jnp.roll(jnp.flip(values, dimension), 1, dimension)


def signed_freq(counter, length):
    shifted = (counter + length // 2) % length - length // 2
    return shifted.astype(jnp.float32) / (length / 2.0)


def body(solid, orientation):
    len_z = solid.shape[2]
    real_part, imag_part = transform(solid.astype(jnp.float32), orientation, "xyz,zk->xyk", len_z)
    real_part, imag_part = (
        lax.all_to_all(real_part, "pz", split_axis=2, concat_axis=1, tiled=True),
        lax.all_to_all(imag_part, "pz", split_axis=2, concat_axis=1, tiled=True),
    )
    len_y = real_part.shape[1]
    real_part, imag_part = transform(real_part, imag_part, "xyz,yk->xzk", len_y)
    real_part, imag_part = (
        lax.all_to_all(real_part, "py", split_axis=2, concat_axis=0, tiled=True),
        lax.all_to_all(imag_part, "py", split_axis=2, concat_axis=0, tiled=True),
    )
    len_x = real_part.shape[0]
    direct_re, direct_im = transform(real_part, imag_part, "xzy,xk->yzk", len_x)
    mirrored = jnp.stack([direct_re, direct_im])
    mirrored = jnp.flip(reflect(mirrored, 3), (1, 2))
    for bit_number in range(lax.axis_size(("py", "pz")).bit_length() - 1):
        mirrored = from_partner(mirrored, ("py", "pz"), bit_number)
    border = from_behind(mirrored[:, -1:, :, :], "py", 1)
    mirrored = jnp.concatenate([border, mirrored[:, :-1, :, :]], 1)
    border = from_behind(mirrored[:, :, -1:, :], "pz", 1)
    mirrored = jnp.concatenate([border, mirrored[:, :, :-1, :]], 2)
    mirr_re = mirrored[0]
    mirr_im = mirrored[1]
    solid_re = (direct_re + mirr_re) / 2.0
    solid_im = (direct_im - mirr_im) / 2.0
    orient_re = (direct_im + mirr_im) / 2.0
    orient_im = (mirr_re - direct_re) / 2.0
    size_y, size_z, size_x = (direct_re.shape[0], direct_re.shape[1], direct_re.shape[2])
    full_y = size_y * lax.axis_size("py")
    full_z = size_z * lax.axis_size("pz")
    index_x = jnp.arange(size_x, dtype=jnp.int32)
    index_y = lax.axis_index("py") * size_y + jnp.arange(size_y, dtype=jnp.int32)
    index_z = lax.axis_index("pz") * size_z + jnp.arange(size_z, dtype=jnp.int32)
    freq_x = signed_freq(index_x, size_x)
    freq_y = signed_freq(index_y, full_y)
    freq_z = signed_freq(index_z, full_z)
    weight = jnp.exp(
        -0.5
        * (freq_y[:, None, None] ** 2 + freq_z[None, :, None] ** 2 + freq_x[None, None, :] ** 2)
    )
    anchor = (
        (index_y[:, None, None] == 0)
        & (index_z[None, :, None] == 0)
        & (index_x[None, None, :] == 0)
    )
    weight = jnp.where(anchor, 0.0, weight)
    scaled = weight / (size_x * full_y * full_z)
    power_solid = scaled * (solid_re * solid_re + solid_im * solid_im)
    power_orient = scaled * (orient_re * orient_re + orient_im * orient_im)
    cross_re = scaled * (solid_re * orient_re + solid_im * orient_im)
    cross_im = scaled * (solid_im * orient_re - solid_re * orient_im)
    return (power_solid, power_orient, jnp.stack([cross_re, cross_im]))


def solution(mesh):
    placed = (P("py", "pz", None), P("py", "pz", None))
    return jax.shard_map(
        body,
        mesh=mesh,
        in_specs=placed,
        out_specs=(P("py", "pz", None), P("py", "pz", None), P(None, "py", "pz", None)),
        check_vma=False,
    )
```

profile of v0, /device:TPU:33, one launch (start us, length us, event | category | flops | bytes accessed | tf_op | source)
XLA Modules:
  0.0 649.7 jit_solution(8086479226529715050)
XLA Ops:
  0.6 4.1 sine_negate_fusion
  4.8 3.5 convolution_bitcast_fusion
  8.3 3.6 convolution_bitcast_fusion.1
  11.9 1.4 slice_add_fusion.2
  13.4 3.9 copy.21
  17.2 4.7 reshape.150
  21.9 6.1 all-to-all-start
  28.0 4.6 copy.23
  32.7 4.7 reshape.152
  37.4 6.0 all-to-all-done
  43.4 5.4 all-to-all-start.1
  49.3 4.3 reduce.1
  53.7 2.7 reshape.151
  56.4 6.6 %copy.37 = f32[16,32,16,32]{1,2,3,0:T(8,128)} copy(f32[16,32,16,32]{1,0,3,2:T(8,128)} %bitcast.103) | data formatting | bytes 2097152 | tf_op jit(solution)/shard_map/all_to_all | solution.py:47
  63.0 3.9 all_to_all.55
  66.9 4.9 fusion.10
  71.8 4.3 reduce
  76.2 2.7 reshape.153
  78.9 6.6 %copy.36 = f32[16,32,16,32]{1,2,3,0:T(8,128)} copy(f32[16,32,16,32]{1,0,3,2:T(8,128)} %bitcast.105) | data formatting | bytes 2097152 | tf_op jit(solution)/shard_map/all_to_all | solution.py:48
  85.5 3.7 all_to_all.59
  89.2 3.6 fusion.9
  93.3 3.7 copy.28
  97.0 4.7 reshape.154
  101.7 10.0 %all-to-all-start.3 = ((f32[16,1,16384]{2,1,0:T(1,128)}), f32[16,1,16384]{2,1,0:T(1,128)S(1)}, u32[]{:S(2)}, u32[]{:S(2)}) async-start(f32[16,1,16384]{2,1,0:T(1,128)} %reshape.154), calls=%async_computation.3 | async-start | bytes 2097152 | tf_op jit(solution)/shard_map/all_to_all | solution.py:54
  111.7 3.7 copy.25
  115.4 4.7 reshape.156
  120.1 22.2 %all-to-all-done.3 = f32[16,1,16384]{2,1,0:T(1,128)S(1)} async-done(((f32[16,1,16384]{2,1,0:T(1,128)}), f32[16,1,16384]{2,1,0:T(1,128)S(1)}, u32[]{:S(2)}, u32[]{:S(2)}) %all-to-all-start.3) | async-done | bytes 1048608 | tf_op jit(solution)/shard_map/all_to_all | solution.py:54
  142.3 3.9 all-to-all-start.2
  146.2 1.7 sine_negate_fusion.1
  148.0 3.1 reduce.3
  151.0 2.7 reshape.155
  153.8 5.6 copy.29
  159.3 3.5 copy.30
  162.9 7.8 %all-to-all-done.2 = f32[16,1,16384]{2,1,0:T(1,128)S(1)} async-done(((f32[16,1,16384]{2,1,0:T(1,128)}), f32[16,1,16384]{2,1,0:T(1,128)S(1)}, u32[]{:S(2)}, u32[]{:S(2)}) %all-to-all-start.2) | async-done | bytes 1048608 | tf_op jit(solution)/shard_map/all_to_all | solution.py:53
  170.7 3.1 reduce.2
  173.7 2.7 reshape.157
  176.5 5.6 copy.26
  182.1 3.8 copy.27
  185.9 1.9 fusion.12
  187.8 1.9 fusion.13
  190.1 1.9 pad_maximum_fusion.1
  192.0 4.2 reverse.2
  196.2 2.2 slice.157
  198.4 2.0 pad_maximum_fusion.2
  200.4 3.8 rev.6
  205.3 4.0 collective-permute-done
  209.3 46.8 %collective-permute-done.1 = f32[2,32,32,256]{3,1,2,0:T(8,128)S(1)} collective-permute-done((f32[2,32,32,256]{3,1,2,0:T(8,128)S(1)}, f32[2,32,32,256]{3,1,2,0:T(8,128)S(1)}, u32[]{:S(2)}, u32[]{:S(2)}) %collective-permute-start.1) | collective-permute-done | bytes 2097184 | tf_op jit(solution)/shard_map/ppermute | solution.py:10
  257.3 44.7 %collective-permute-done.2 = f32[2,32,32,256]{3,1,2,0:T(8,128)S(1)} collective-permute-done((f32[2,32,32,256]{3,1,2,0:T(8,128)S(1)}, f32[2,32,32,256]{3,1,2,0:T(8,128)S(1)}, u32[]{:S(2)}, u32[]{:S(2)}) %collective-permute-start.2) | collective-permute-done | bytes 2097184 | tf_op jit(solution)/shard_map/ppermute | solution.py:10
  302.0 2.7 collective-permute-start.3
  304.7 43.8 %collective-permute-done.3 = f32[2,32,32,256]{3,1,2,0:T(8,128)S(1)} collective-permute-done((f32[2,32,32,256]{3,1,2,0:T(8,128)S(1)}, f32[2,32,32,256]{3,1,2,0:T(8,128)S(1)}, u32[]{:S(2)}, u32[]{:S(2)}) %collective-permute-start.3) | collective-permute-done | bytes 2097184 | tf_op jit(solution)/shard_map/ppermute | solution.py:10
  348.7 43.9 %collective-permute-done.4 = f32[2,32,32,256]{3,1,2,0:T(8,128)S(1)} collective-permute-done((f32[2,32,32,256]{3,1,2,0:T(8,128)S(1)}, f32[2,32,32,256]{3,1,2,0:T(8,128)S(1)}, u32[]{:S(2)}, u32[]{:S(2)}) %collective-permute-start.4) | collective-permute-done | bytes 2097184 | tf_op jit(solution)/shard_map/ppermute | solution.py:10
  392.6 1.9 collective-permute-start.5
  394.5 43.1 %collective-permute-done.5 = f32[2,32,32,256]{3,1,2,0:T(8,128)S(1)} collective-permute-done((f32[2,32,32,256]{3,1,2,0:T(8,128)S(1)}, f32[2,32,32,256]{3,1,2,0:T(8,128)S(1)}, u32[]{:S(2)}, u32[]{:S(2)}) %collective-permute-start.5) | collective-permute-done | bytes 2097184 | tf_op jit(solution)/shard_map/ppermute | solution.py:10
  437.6 1.8 collective-permute-start.6
  439.4 89.7 %collective-permute-done.6 = f32[2,32,32,256]{3,1,2,0:T(8,128)} collective-permute-done((f32[2,32,32,256]{3,1,2,0:T(8,128)S(1)}, f32[2,32,32,256]{3,1,2,0:T(8,128)}, u32[]{:S(2)}, u32[]{:S(2)}) %collective-permute-start.6) | collective-permute-done | bytes 2097184 | tf_op jit(solution)/shard_map/ppermute | solution.py:10
  530.4 65.2 %collective-permute-done.7 = f32[2,32,32,256]{3,1,2,0:T(8,128)} collective-permute-done((f32[2,32,32,256]{3,1,2,0:T(8,128)}, f32[2,32,32,256]{3,1,2,0:T(8,128)}, u32[]{:S(2)}, u32[]{:S(2)}) %collective-permute-start.7) | collective-permute-done | bytes 2097184 | tf_op jit(solution)/shard_map/ppermute | solution.py:10
  596.7 34.3 %collective-permute-done.8 = f32[2,1,32,256]{3,1,2,0:T(1,128)S(1)} collective-permute-done((f32[2,1,32,256]{3,1,2,0:T(1,128)S(1)}, f32[2,1,32,256]{3,1,2,0:T(1,128)S(1)}, u32[]{:S(2)}, u32[]{:S(2)}) %collective-permute-start.8) | collective-permute-done | bytes 65568 | tf_op jit(solution)/shard_map/ppermute | solution.py:15
  631.9 6.7 %collective-permute-start.9 = (f32[2,32,1,256]{3,1,2,0:T(8,128)S(1)}, f32[2,32,1,256]{3,1,2,0:T(8,128)S(1)}, u32[]{:S(2)}, u32[]{:S(2)}) collective-permute-start(f32[2,32,1,256]{3,1,2,0:T(8,128)S(1)} %pad_maximum_fusion.7), channel_id=1, source_target_pairs={{0,1},{1,2},{2,3},{3,4},{4,5},{5,6},{6,7},{7,8},{8,9},{9,10},{10,1... | collective-permute-start | bytes 196616 | tf_op jit(solution)/shard_map/ppermute | solution.py:15
  638.6 1.3 collective-permute-done.9
  640.0 1.9 fusion
  641.8 1.5 multiply_bitcast_fusion.1
  643.5 2.5 copy.33
  646.0 1.6 copy.31
  647.6 1.6 copy.32
  (32 shorter events, 7.3 us)
Async XLA Ops:
  0.6 4.1 copy-start
  4.8 3.6 copy-start.5
  21.9 21.4 %all-to-all-start = ((f32[16,1,16384]{2,1,0:T(1,128)}), f32[16,1,16384]{2,1,0:T(1,128)S(1)}, u32[]{:S(2)}, u32[]{:S(2)}) async-start(f32[16,1,16384]{2,1,0:T(1,128)} %reshape.150), calls=%async_computation | async-start | bytes 2097152 | tf_op jit(solution)/shard_map/all_to_all | solution.py:47
  43.4 5.5 copy-start.3
  43.4 28.5 %all-to-all-start.1 = ((f32[16,1,16384]{2,1,0:T(1,128)}), f32[16,1,16384]{2,1,0:T(1,128)}, u32[]{:S(2)}, u32[]{:S(2)}) async-start(f32[16,1,16384]{2,1,0:T(1,128)} %reshape.152), calls=%async_computation.1 | async-start | bytes 2097152 | tf_op jit(solution)/shard_map/all_to_all | solution.py:48
  89.2 3.6 copy-start.2
  101.7 40.6 %all-to-all-start.3 = ((f32[16,1,16384]{2,1,0:T(1,128)}), f32[16,1,16384]{2,1,0:T(1,128)S(1)}, u32[]{:S(2)}, u32[]{:S(2)}) async-start(f32[16,1,16384]{2,1,0:T(1,128)} %reshape.154), calls=%async_computation.3 | async-start | bytes 2097152 | tf_op jit(solution)/shard_map/all_to_all | solution.py:54
  142.3 28.3 %all-to-all-start.2 = ((f32[16,1,16384]{2,1,0:T(1,128)}), f32[16,1,16384]{2,1,0:T(1,128)S(1)}, u32[]{:S(2)}, u32[]{:S(2)}) async-start(f32[16,1,16384]{2,1,0:T(1,128)} %reshape.156), calls=%async_computation.2 | async-start | bytes 2097152 | tf_op jit(solution)/shard_map/all_to_all | solution.py:53
  182.1 3.8 copy-start.4
  204.2 5.1 collective-permute-start
  209.3 46.8 %collective-permute-start.1 = (f32[2,32,32,256]{3,1,2,0:T(8,128)S(1)}, f32[2,32,32,256]{3,1,2,0:T(8,128)S(1)}, u32[]{:S(2)}, u32[]{:S(2)}) collective-permute-start(f32[2,32,32,256]{3,1,2,0:T(8,128)S(1)} %collective-permute-done), channel_id=1, source_target_pairs={{0,2},{1,3},{2,0},{3,1},{4,6},{5,7},{6,4},{7,5},{8,10},{9,11},{10,... | collective-permute-start | bytes 6291464 | tf_op jit(solution)/shard_map/ppermute | solution.py:10
  256.1 45.9 %collective-permute-start.2 = (f32[2,32,32,256]{3,1,2,0:T(8,128)S(1)}, f32[2,32,32,256]{3,1,2,0:T(8,128)S(1)}, u32[]{:S(2)}, u32[]{:S(2)}) collective-permute-start(f32[2,32,32,256]{3,1,2,0:T(8,128)S(1)} %collective-permute-done.1), channel_id=1, source_target_pairs={{0,4},{1,5},{2,6},{3,7},{4,0},{5,1},{6,2},{7,3},{8,12},{9,13},{10,... | collective-permute-start | bytes 6291464 | tf_op jit(solution)/shard_map/ppermute | solution.py:10
  302.0 46.5 %collective-permute-start.3 = (f32[2,32,32,256]{3,1,2,0:T(8,128)S(1)}, f32[2,32,32,256]{3,1,2,0:T(8,128)S(1)}, u32[]{:S(2)}, u32[]{:S(2)}) collective-permute-start(f32[2,32,32,256]{3,1,2,0:T(8,128)S(1)} %collective-permute-done.2), channel_id=1, source_target_pairs={{0,8},{1,9},{2,10},{3,11},{4,12},{5,13},{6,14},{7,15},{8,0},{9,1},... | collective-permute-start | bytes 6291464 | tf_op jit(solution)/shard_map/ppermute | solution.py:10
  348.5 44.1 %collective-permute-start.4 = (f32[2,32,32,256]{3,1,2,0:T(8,128)S(1)}, f32[2,32,32,256]{3,1,2,0:T(8,128)S(1)}, u32[]{:S(2)}, u32[]{:S(2)}) collective-permute-start(f32[2,32,32,256]{3,1,2,0:T(8,128)S(1)} %collective-permute-done.3), channel_id=1, source_target_pairs={{0,16},{1,17},{2,18},{3,19},{4,20},{5,21},{6,22},{7,23},{8,24},{9,... | collective-permute-start | bytes 6291464 | tf_op jit(solution)/shard_map/ppermute | solution.py:10
  392.6 45.0 %collective-permute-start.5 = (f32[2,32,32,256]{3,1,2,0:T(8,128)S(1)}, f32[2,32,32,256]{3,1,2,0:T(8,128)S(1)}, u32[]{:S(2)}, u32[]{:S(2)}) collective-permute-start(f32[2,32,32,256]{3,1,2,0:T(8,128)S(1)} %collective-permute-done.4), channel_id=1, source_target_pairs={{0,32},{1,33},{2,34},{3,35},{4,36},{5,37},{6,38},{7,39},{8,40},{9,... | collective-permute-start | bytes 6291464 | tf_op jit(solution)/shard_map/ppermute | solution.py:10
  437.6 91.5 %collective-permute-start.6 = (f32[2,32,32,256]{3,1,2,0:T(8,128)S(1)}, f32[2,32,32,256]{3,1,2,0:T(8,128)}, u32[]{:S(2)}, u32[]{:S(2)}) collective-permute-start(f32[2,32,32,256]{3,1,2,0:T(8,128)S(1)} %collective-permute-done.5), channel_id=1, source_target_pairs={{0,64},{1,65},{2,66},{3,67},{4,68},{5,69},{6,70},{7,71},{8,72},{9,... | collective-permute-start | bytes 6291464 | tf_op jit(solution)/shard_map/ppermute | solution.py:10
  529.1 66.4 %collective-permute-start.7 = (f32[2,32,32,256]{3,1,2,0:T(8,128)}, f32[2,32,32,256]{3,1,2,0:T(8,128)}, u32[]{:S(2)}, u32[]{:S(2)}) collective-permute-start(f32[2,32,32,256]{3,1,2,0:T(8,128)} %collective-permute-done.6), channel_id=1, source_target_pairs={{0,128},{1,129},{2,130},{3,131},{4,132},{5,133},{6,134},{7,135},{8... | collective-permute-start | bytes 6291464 | tf_op jit(solution)/shard_map/ppermute | solution.py:10
  596.6 34.4 %collective-permute-start.8 = (f32[2,1,32,256]{3,1,2,0:T(1,128)S(1)}, f32[2,1,32,256]{3,1,2,0:T(1,128)S(1)}, u32[]{:S(2)}, u32[]{:S(2)}) collective-permute-start(f32[2,1,32,256]{3,1,2,0:T(1,128)S(1)} %slice.101), channel_id=1, source_target_pairs={{0,16},{16,32},{32,48},{48,64},{64,80},{80,96},{96,112},{112,128},... | collective-permute-start | bytes 196616 | tf_op jit(solution)/shard_map/ppermute | solution.py:15
  631.9 8.0 %collective-permute-start.9 = (f32[2,32,1,256]{3,1,2,0:T(8,128)S(1)}, f32[2,32,1,256]{3,1,2,0:T(8,128)S(1)}, u32[]{:S(2)}, u32[]{:S(2)}) collective-permute-start(f32[2,32,1,256]{3,1,2,0:T(8,128)S(1)} %pad_maximum_fusion.7), channel_id=1, source_target_pairs={{0,1},{1,2},{2,3},{3,4},{4,5},{5,6},{6,7},{7,8},{8,9},{9,10},{10,1... | collective-permute-start | bytes 196616 | tf_op jit(solution)/shard_map/ppermute | solution.py:15
  646.0 3.2 copy-start.1
where the time goes:
time: 662 us; the launch traced here: 650 us
  waiting for transfers between devices  453 us (68%)
  local copies, waits for them, and re-layouts  102 us (15%)
  starting transfers between devices  42.1 us (6%)
  other arithmetic  31.5 us (5%)
  matrix products  19.3 us (3%)
    ppermute x8, waiting for transfers between devices, from_partner(): lax.ppermute(shard, axis, [(i, i ^ 1 << apart) for i in range(lax.axis_si...  381 us
    unnamed x25, local copies, waits for them, and re-layouts  41.8 us
    ppermute x2, waiting for transfers between devices, from_behind(): lax.ppermute(shard, axis, [(i, (i + by) % devices) for i in range(devices)])  35.7 us
    all_to_all x1, waiting for transfers between devices, body(): lax.all_to_all(imag_part, 'py', split_axis=2, concat_axis=0, tiled=True)  22.2 us
  transfers between devices with their start and end apart: 14, of which 13 were waited for; matrix products, arithmetic and copies ran while one was open for 8% of the time, Pallas kernels for 0%

commit v1 on v0

v1 whole, which is shorter than its diff:
```python
import jax
import jax.numpy as jnp
import numpy as np
from jax import lax
from jax.experimental import pallas as pl
from jax.experimental.pallas import tpu as pltpu
from jax.sharding import PartitionSpec as P

F32 = jnp.float32
BF16 = jnp.bfloat16
LANES = 128
VMEM_LIMIT = 56 * 1024 * 1024


def two_parts(table):
    high = np.asarray(table, np.float32).astype(jnp.bfloat16)
    low = (np.asarray(table, np.float64) - high.astype(np.float64)).astype(np.float32).astype(jnp.bfloat16)
    return high, low


def cos_sin(rows, columns, length):
    angles = (np.outer(rows, columns) % length) * (2.0 * np.pi / length)
    return np.cos(angles), np.sin(angles)


def first_kz(place):
    return 32 * place if place < 8 else 32 * (15 - place) + 16


def z_tables():
    z = np.arange(512)
    regular, extra = [], []
    for place in range(16):
        cos, sin = cos_sin(z, first_kz(place) + np.arange(17), 512)
        regular += [cos[:, :16], -sin[:, :16]]
        extra += [cos[:, 16:], -sin[:, 16:]]
    return two_parts(np.concatenate(regular + extra * 4, 1))


def y_tables():
    n = np.arange(512)
    cos, sin = cos_sin(n, n, 512)
    return two_parts(np.concatenate([cos, sin], 0))


def x_tables():
    half, source, low = np.meshgrid(np.arange(2), np.arange(16), np.arange(8), indexing="ij")
    x = (source * 16 + half * 8 + low).reshape(-1)
    cos, sin = cos_sin(x, np.arange(256), 256)
    return two_parts(np.concatenate([cos, sin], 1))


def split(values):
    high = values.astype(BF16)
    return high, (values - high.astype(F32)).astype(BF16)


def dot(a, b):
    return jnp.dot(a, b, preferred_element_type=F32)


def lane_of(shape):
    return lax.broadcasted_iota(jnp.int32, shape, len(shape) - 1)


def permuted(values, source_lane):
    return jnp.take_along_axis(values, source_lane, axis=1, mode="promise_in_bounds")


def z_kernel(solid_ref, orient_ref, high_ref, low_ref, out_ref):
    size_y = solid_ref.shape[1]
    rows = 8 * size_y
    high, low = high_ref[...], low_ref[...]
    solid = solid_ref[...].reshape(2 * rows, 512).astype(F32).astype(BF16)
    orient, rest = split(orient_ref[...].reshape(2 * rows, 512))
    solid_z = dot(solid, high) + dot(solid, low)
    orient_z = dot(orient, high) + (dot(orient, low) + dot(rest, high))
    pieces = (solid_z[:rows], orient_z[:rows], solid_z[rows:], orient_z[rows:])
    lane = lane_of((rows, LANES))
    group = lane // 32

    def gathered(parts):
        return jnp.where(group == 0, parts[0], jnp.where(group == 1, parts[1], jnp.where(group == 2, parts[2], parts[3])))

    for tile in range(4):
        columns = [piece[:, LANES * tile : LANES * (tile + 1)] for piece in pieces]
        for q in range(4):
            moved = [columns[c] if c == q else pltpu.roll(columns[c], 32 * (c - q) % LANES, 1) for c in range(4)]
            out_ref[4 * tile + q, 0:8] = gathered(moved).reshape(8, size_y, LANES)
    extra = gathered([piece[:, 512:640] for piece in pieces])
    spot = lane_of((size_y, LANES)) % 16
    for place in range(16):
        spread = permuted(extra, group * 32 + 2 * place + lane // 16 % 2)
        total = jnp.zeros((size_y, LANES), F32)
        for k in range(8):
            total = jnp.where(spot == k, spread[k * size_y : (k + 1) * size_y], total)
        out_ref[place, 8] = total


def y_kernel(data_ref, extra_ref, high_ref, low_ref, out_ref, extra_y_ref):
    high, low = high_ref[...], low_ref[...]
    lane = lane_of((512, LANES))
    sign = jnp.where(lane // 16 % 2 == 0, 1.0, -1.0).astype(F32)
    swap = lane ^ 16
    back = lane // 16 * 16 + (16 - lane % 16) % 16

    def transformed(values):
        first, rest = split(values)
        return dot(high, first) + (dot(high, rest) + dot(low, first))

    def turned(products):
        return permuted(products, swap) * sign

    @pl.when(pl.program_id(0) == 0)
    def _():
        products = transformed(extra_ref[...].reshape(512, LANES))
        extra_y_ref[...] = (products[:512] - turned(products[512:])) * sign

    per_step = data_ref.shape[1]
    values = jnp.concatenate([data_ref[:, k].reshape(512, LANES) for k in range(per_step)], 1)
    products = transformed(values)
    for k in range(per_step):
        cos_part = products[:512, LANES * k : LANES * (k + 1)]
        sin_part = turned(products[512:, LANES * k : LANES * (k + 1)])
        out_ref[:, 0, k] = (cos_part + sin_part).reshape(16, 32, LANES)
        mirrored = permuted((cos_part - sin_part) * sign, back)
        x8 = pl.program_id(0) * per_step + k
        border = pltpu.roll(extra_y_ref[...], (LANES - x8) % LANES, 1)
        out_ref[:, 1, k] = jnp.where(lane % 16 == 0, border, mirrored).reshape(16, 32, LANES)


def signed_freq(counter, length):
    shifted = (counter + length // 2) % length - length // 2
    return shifted.astype(F32) / (length / 2.0)


def x_kernel(place_ref, data_ref, high_ref, low_ref, solid_ref, orient_ref, cross_ref, first_ref, rest_ref):
    size_y = solid_ref.shape[0]
    pz = place_ref[1]
    flip = (pz >= 8).astype(jnp.int32)
    for ky in range(size_y):
        for half in range(2):
            rows = [data_ref[source, half ^ flip, pl.ds(ky, 8, stride=size_y), :] for source in range(16)]
            turned = jnp.concatenate(rows, 0).T
            joined = jnp.concatenate([turned[:64], turned[64:]], 1)
            first, rest = split(joined)
            start = ky * 128 + half * 64
            first_ref[start : start + 64] = first
            rest_ref[start : start + 64] = rest
    high, low = high_ref[...], low_ref[...]
    products = dot(first_ref[...], high) + (dot(first_ref[...], low) + dot(rest_ref[...], high))

    kx = lax.broadcasted_iota(jnp.int32, (32, 256), 1)
    kz = lax.broadcasted_iota(jnp.int32, (32, 256), 0) + pz * 32
    freq = signed_freq(kx, 256) ** 2 + signed_freq(kz, 512) ** 2
    plane = jnp.exp(-0.5 * freq) * (1.0 / 67108864.0)
    first_ky = place_ref[0] * 32 + pl.program_id(0) * size_y
    for ky in range(size_y):
        index = jnp.full((32, 256), first_ky + ky, jnp.int32)
        weight = plane * jnp.exp(-0.5 * signed_freq(index[:1], 512) ** 2)
        weight = jnp.where((kx == 0) & (kz == 0) & (index == 0), 0.0, weight)
        for half in range(2):
            start = ky * 128 + half * 64
            cos_part = [products[start + 16 * i : start + 16 * (i + 1), :256] for i in range(4)]
            sin_part = [products[start + 16 * i : start + 16 * (i + 1), 256:] for i in range(4)]
            solid_re = cos_part[0] + sin_part[1]
            solid_im = cos_part[1] - sin_part[0]
            orient_re = cos_part[2] + sin_part[3]
            orient_im = cos_part[3] - sin_part[2]
            scaled = weight[16 * half : 16 * (half + 1)]
            where = pl.ds(16 * half, 16)
            solid_ref[ky, where] = scaled * (solid_re * solid_re + solid_im * solid_im)
            orient_ref[ky, where] = scaled * (orient_re * orient_re + orient_im * orient_im)
            cross_ref[0, ky, where] = scaled * (solid_re * orient_re + solid_im * orient_im)
            cross_ref[1, ky, where] = scaled * (solid_im * orient_re - solid_re * orient_im)


def whole(shape):
    return pl.BlockSpec(shape, lambda *_: (0,) * len(shape))


def body(solid, orientation):
    params = pltpu.CompilerParams(vmem_limit_bytes=VMEM_LIMIT, dimension_semantics=("arbitrary",))
    z_high, z_low = z_tables()
    step_y = 8
    field = pl.pallas_call(
        z_kernel,
        grid=(32 // step_y,),
        in_specs=[
            pl.BlockSpec((16, step_y, 512), lambda i: (0, i, 0)),
            pl.BlockSpec((16, step_y, 512), lambda i: (0, i, 0)),
            whole(z_high.shape),
            whole(z_low.shape),
        ],
        out_specs=pl.BlockSpec((16, 9, step_y, LANES), lambda i: (0, 0, i, 0)),
        out_shape=jax.ShapeDtypeStruct((16, 9, 32, LANES), F32),
        compiler_params=params,
        name="z_transform",
    )(solid, orientation, z_high, z_low)
    field = lax.all_to_all(field.reshape(16, 9 * 32, LANES), "pz", 0, 0, tiled=True).reshape(16, 9, 32, LANES)

    y_high, y_low = y_tables()
    per_step = 2
    field = pl.pallas_call(
        y_kernel,
        grid=(8 // per_step,),
        in_specs=[
            pl.BlockSpec((16, per_step, 32, LANES), lambda i: (0, i, 0, 0)),
            pl.BlockSpec((16, 1, 32, LANES), lambda i: (0, 8, 0, 0)),
            whole(y_high.shape),
            whole(y_low.shape),
        ],
        out_specs=pl.BlockSpec((16, 2, per_step, 32, LANES), lambda i: (0, 0, i, 0, 0)),
        out_shape=jax.ShapeDtypeStruct((16, 2, 8, 32, LANES), F32),
        scratch_shapes=[pltpu.VMEM((512, LANES), F32)],
        compiler_params=params,
        name="y_transform",
    )(field, field, y_high, y_low)
    groups = [[py * 16 + pz for py in range(16) for pz in (low, 15 - low)] for low in range(8)]
    field = lax.all_to_all(
        field.reshape(32, 8 * 32, LANES), ("py", "pz"), 0, 0, tiled=True, axis_index_groups=groups
    ).reshape(16, 2, 8, 32, LANES)

    x_high, x_low = x_tables()
    step_ky = 8
    place = jnp.stack([lax.axis_index("py"), lax.axis_index("pz")]).astype(jnp.int32)
    out_spec = pl.BlockSpec((step_ky, 32, 256), lambda i: (i, 0, 0))
    cross_spec = pl.BlockSpec((2, step_ky, 32, 256), lambda i: (0, i, 0, 0))
    out = jax.ShapeDtypeStruct((32, 32, 256), F32)

    def with_rows(place_ref, data_ref, *refs):
        x_kernel(place_ref, data_ref.reshape(16, 2, 8 * step_ky, LANES), *refs)

    return tuple(
        pl.pallas_call(
            with_rows,
            grid=(32 // step_ky,),
            in_specs=[
                pl.BlockSpec(memory_space=pltpu.SMEM),
                pl.BlockSpec((16, 2, 8, step_ky, LANES), lambda i: (0, 0, 0, i, 0)),
                whole(x_high.shape),
                whole(x_low.shape),
            ],
            out_specs=[out_spec, out_spec, cross_spec],
            out_shape=[out, out, jax.ShapeDtypeStruct((2, 32, 32, 256), F32)],
            scratch_shapes=[pltpu.VMEM((step_ky * 128, 256), BF16)] * 2,
            compiler_params=params,
            name="x_transform",
        )(place, field, x_high, x_low)
    )


def solution(mesh):
    placed = (P("py", "pz", None), P("py", "pz", None))
    return jax.shard_map(
        body,
        mesh=mesh,
        in_specs=placed,
        out_specs=(P("py", "pz", None), P("py", "pz", None), P(None, "py", "pz", None)),
        check_vma=False,
    )
```

time: 662 us -> 170 us (0.26); the launches traced: 650 us -> 169 us
  waiting for transfers between devices: 453 us -> 97.5 us
  local copies, waits for them, and re-layouts: 102 us -> 0 us
  blocking collectives: 0 us -> 35.8 us
  starting transfers between devices: 42.1 us -> 10.5 us
  other arithmetic: 31.5 us -> 0.59 us
  Pallas kernels: 0 us -> 24.2 us
  matrix products: 19.3 us -> 0 us
    ppermute x10 -> x0, waiting for transfers between devices: 417 us -> none  [the longest x8 381 us: from_partner(): lax.ppermute(shard, axis, [(i, i ^ 1 << apart) for i in range(lax.axis_si...]
    all_to_all x4 -> x1, waiting for transfers between devices: 36 us -> 97.5 us  [body(): lax.all_to_all(field.reshape(32, 8 * 32, LANES), ('py', 'pz'), 0, 0, tile...]
    unnamed x25 -> x0, local copies, waits for them, and re-layouts: 41.8 us -> none
    all_to_all x9 -> x0, local copies, waits for them, and re-layouts: 39.8 us -> none  [the longest x3 10.8 us: body(): lax.all_to_all(imag_part, 'pz', split_axis=2, concat_axis=1, tiled=True)]
    all_to_all x0 -> x1, blocking collectives: none -> 35.8 us  [body(): lax.all_to_all(field.reshape(16, 9 * 32, LANES), 'pz', 0, 0, tiled=True)]
    pallas_call x0 -> x3, Pallas kernels: none -> 24.2 us  [the longest x1 9.72 us: body(): pl.pallas_call(y_kernel, grid=(8 // per_step,), in_specs=[pl.BlockSpec((1...]
    ppermute x10 -> x0, starting transfers between devices: 16.7 us -> none  [the longest x8 9.92 us: from_partner(): lax.ppermute(shard, axis, [(i, i ^ 1 << apart) for i in range(lax.axis_si...]
    dot_general x4 -> x0, matrix products: 15.6 us -> none  [the longest x2 8.45 us: transform(): first = jnp.einsum(form, real_part, joined, precision=lax.Precision.HIGHEST)]
  transfers between devices with their start and end apart: 14 -> 1, of which waited for: 13 -> 1; matrix products, arithmetic and copies ran while one was open for 8% -> 0% of each run, Pallas kernels for 0% -> 0%
where the time goes in v1:
time: 170 us; the launch traced here: 169 us
  waiting for transfers between devices  97.5 us (57%)
  blocking collectives  35.8 us (21%)
  Pallas kernels  24.2 us (14%)
  starting transfers between devices  10.5 us (6%)
    all_to_all x1, waiting for transfers between devices, body(): lax.all_to_all(field.reshape(32, 8 * 32, LANES), ('py', 'pz'), 0, 0, tile...  97.5 us
    all_to_all x1, blocking collectives, body(): lax.all_to_all(field.reshape(16, 9 * 32, LANES), 'pz', 0, 0, tiled=True)  35.8 us
    all_to_all x1, starting transfers between devices, body(): lax.all_to_all(field.reshape(32, 8 * 32, LANES), ('py', 'pz'), 0, 0, tile...  10.5 us
    pallas_call x1, Pallas kernels, body(): pl.pallas_call(y_kernel, grid=(8 // per_step,), in_specs=[pl.BlockSpec((1...  9.72 us
    pallas_call x1, Pallas kernels, body(): pl.pallas_call(with_rows, grid=(32 // step_ky,), in_specs=[pl.BlockSpec(m...  7.27 us
    pallas_call x1, Pallas kernels, body(): pl.pallas_call(z_kernel, grid=(32 // step_y,), in_specs=[pl.BlockSpec((16...  7.2 us
  transfers between devices with their start and end apart: 1, of which 1 were waited for; matrix products, arithmetic and copies ran while one was open for 0% of the time, Pallas kernels for 0%

profile of v1, /device:TPU:33, one launch (start us, length us, event | category | flops | bytes accessed | tf_op | source)
XLA Modules:
  0.0 169.2 jit_solution(3464139853165799539)
XLA Ops:
  0.6 7.2 %z_transform.1 = f32[16,9,32,128]{3,2,1,0:T(8,128)} custom-call(s32[16,32,512]{2,1,0:T(8,128)} %solid_ref.1, f32[16,32,512]{2,1,0:T(8,128)} %orient_ref.1, bf16[512,640]{1,0:T(8,128)(2,1)} %constant.19.clone.high_ref, bf16[512,640]{1,0:T(8,128)(2,1)} %constant.20.clone.low_ref), custom_call_target="tpu_custom_call" | custom-call | tf_op jit(solution)/shard_map/z_transform/pallas_call | solution.py:186
  7.8 35.8 %all_to_all.10 = f32[16,288,128]{2,1,0:T(8,128)} all-to-all(f32[16,288,128]{2,1,0:T(8,128)} %bitcast.9), channel_id=1, replica_groups=mesh['py'=16,'pz'=16] {'pz'}, dimensions={0} | all-to-all | bytes 4718592 | tf_op jit(solution)/shard_map/all_to_all | solution.py:200
  43.7 9.7 %y_transform.1 = f32[16,2,8,32,128]{4,3,2,1,0:T(8,128)} custom-call(f32[16,9,32,128]{3,2,1,0:T(8,128)} %bitcast.6, f32[16,9,32,128]{3,2,1,0:T(8,128)} %bitcast.7, bf16[1024,512]{1,0:T(8,128)(2,1)} %constant.21.clone.high_ref, bf16[1024,512]{1,0:T(8,128)(2,1)} %constant.22.clone.low_ref), custom_call_target="tpu_custom_call" | custom-call | tf_op jit(solution)/shard_map/y_transform/pallas_call | solution.py:204
  53.4 10.5 %all-to-all-start.1 = ((f32[32,256,128]{2,1,0:T(8,128)}), f32[32,256,128]{2,1,0:T(8,128)}, u32[]{:S(2)}, u32[]{:S(2)}) async-start(f32[32,256,128]{2,1,0:T(8,128)} %bitcast.8), calls=%async_computation.1 | async-start | bytes 8388608 | tf_op jit(solution)/shard_map/all_to_all | solution.py:220
  63.9 0.6 pad_add_fusion.place_ref
  64.5 97.5 %all-to-all-done.1 = f32[32,256,128]{2,1,0:T(8,128)} async-done(((f32[32,256,128]{2,1,0:T(8,128)}), f32[32,256,128]{2,1,0:T(8,128)}, u32[]{:S(2)}, u32[]{:S(2)}) %all-to-all-start.1) | async-done | bytes 4194336 | tf_op jit(solution)/shard_map/all_to_all | solution.py:220
  161.9 7.3 %x_transform.1 = (f32[32,32,256]{2,1,0:T(8,128)}, f32[32,32,256]{2,1,0:T(8,128)}, f32[2,32,32,256]{3,2,1,0:T(8,128)}) custom-call(s32[2]{0:T(128)} %pad_add_fusion.place_ref, f32[16,2,8,32,128]{4,3,2,1,0:T(8,128)} %bitcast.5.data_ref, bf16[256,512]{1,0:T(8,128)(2,1)} %constant.23.clone.refs_0_, bf16[256,512]{1,0:T(8,128)(2,1)} %constant.24.clone.refs_1_), custom_call_target="tpu_custom_call" | custom-call | tf_op jit(solution)/shard_map/x_transform/pallas_call | solution.py:235
Async XLA Ops:
  53.4 108.6 %all-to-all-start.1 = ((f32[32,256,128]{2,1,0:T(8,128)}), f32[32,256,128]{2,1,0:T(8,128)}, u32[]{:S(2)}, u32[]{:S(2)}) async-start(f32[32,256,128]{2,1,0:T(8,128)} %bitcast.8), calls=%async_computation.1 | async-start | bytes 8388608 | tf_op jit(solution)/shard_map/all_to_all | solution.py:220

commit v2 on v1

v2 whole, which is shorter than its diff:
```python
import jax
import jax.numpy as jnp
import numpy as np
from jax import lax
from jax.experimental import pallas as pl
from jax.experimental.pallas import tpu as pltpu
from jax.sharding import PartitionSpec as P

F32 = jnp.float32
BF16 = jnp.bfloat16
LANES = 128
VMEM_LIMIT = 36 * 1024 * 1024
STEP_Y = 8
STEP_KY = 8


def two_parts(table):
    high = np.asarray(table, np.float32).astype(jnp.bfloat16)
    low = (np.asarray(table, np.float64) - high.astype(np.float64)).astype(np.float32).astype(jnp.bfloat16)
    return high, low


def cos_sin(rows, columns, length):
    angles = (np.outer(rows, columns) % length) * (2.0 * np.pi / length)
    return np.cos(angles), np.sin(angles)


def first_kz(place):
    return 32 * place if place < 8 else 32 * (15 - place) + 16


def z_tables():
    z = np.arange(512)
    regular, extra = [], []
    for place in range(16):
        cos, sin = cos_sin(z, first_kz(place) + np.arange(17), 512)
        regular += [cos[:, :16], -sin[:, :16]]
        extra += [cos[:, 16:], -sin[:, 16:]]
    return two_parts(np.concatenate(regular + extra * 4, 1))


def y_tables():
    n = np.arange(512)
    cos, sin = cos_sin(n, n, 512)
    return two_parts(np.concatenate([cos, sin], 0))


def x_tables():
    half, source, low = np.meshgrid(np.arange(2), np.arange(16), np.arange(8), indexing="ij")
    x = (source * 16 + half * 8 + low).reshape(-1)
    cos, sin = cos_sin(x, np.arange(256), 256)
    return two_parts(np.concatenate([cos, sin], 1))


def split(values):
    high = values.astype(BF16)
    return high, (values - high.astype(F32)).astype(BF16)


def dot(a, b):
    return jnp.dot(a, b, preferred_element_type=F32)


def lane_of(shape):
    return lax.broadcasted_iota(jnp.int32, shape, len(shape) - 1)


def permuted(values, source_lane):
    return jnp.take_along_axis(values, source_lane, axis=1, mode="promise_in_bounds")


def z_kernel(solid_ref, orient_ref, high_ref, low_ref, out_ref):
    size_y = STEP_Y
    rows = 8 * size_y
    chunks = 32 // size_y
    i = pl.program_id(0)
    high, low = high_ref[...], low_ref[...]
    lane = lane_of((rows, LANES))
    group = lane // 32

    def gathered(items):
        return jnp.where(group == 0, items[0], jnp.where(group == 1, items[1], jnp.where(group == 2, items[2], items[3])))

    spot = lane_of((size_y, LANES)) % 16
    solid = solid_ref[...].reshape(2 * rows, 512).astype(F32).astype(BF16)
    orient, rest = split(orient_ref[...].reshape(2 * rows, 512))
    solid_z = dot(solid, high) + dot(solid, low)
    orient_z = dot(orient, high) + (dot(orient, low) + dot(rest, high))
    pieces = (solid_z[:rows], orient_z[:rows], solid_z[rows:], orient_z[rows:])
    first = pl.multiple_of(i * size_y, 8)
    for tile in range(4):
        columns = [piece[:, LANES * tile : LANES * (tile + 1)] for piece in pieces]
        for q in range(4):
            moved = [columns[c] if c == q else pltpu.roll(columns[c], 32 * (c - q) % LANES, 1) for c in range(4)]
            ready = gathered(moved)
            for k in range(8):
                out_ref[4 * tile + q, pl.ds(32 * k + first, size_y)] = ready[k * size_y : (k + 1) * size_y]
    extra = gathered([piece[:, 512:640] for piece in pieces])
    shift = 8 * (2 * i // chunks)
    place_rows = pl.ds(pl.multiple_of(256 + i * size_y % 16, 8), size_y)
    for place in range(16):
        spread = permuted(extra, group * 32 + 2 * place + lane // 16 % 2)
        total = jnp.where(shift == 0, 0.0, out_ref[place, place_rows])
        for k in range(8):
            total = jnp.where(spot == k + shift, spread[k * size_y : (k + 1) * size_y], total)
        out_ref[place, place_rows] = total


def y_kernel(data_ref, high_ref, low_ref, out_ref):
    high, low = high_ref[...], low_ref[...]
    lane = lane_of((512, LANES))
    sign = jnp.where(lane // 16 % 2 == 0, 1.0, -1.0).astype(F32)
    swap = lane ^ 16
    back = lane // 16 * 16 + (16 - lane % 16) % 16

    def transformed(values):
        first, rest = split(values)
        return dot(high, first) + (dot(high, rest) + dot(low, first))

    def turned(products):
        return permuted(products, swap) * sign

    border = data_ref[:, 256:272]
    moved = pltpu.roll(border.reshape(256, LANES), LANES - 8, 1).reshape(16, 16, LANES)
    products = transformed(jnp.concatenate([border, moved], 1).reshape(512, LANES))
    extra = (products[:512] - turned(products[512:])) * sign
    for step in range(4):
        pair = (2 * step, 2 * step + 1)
        values = jnp.concatenate([data_ref[:, 32 * k : 32 * (k + 1)].reshape(512, LANES) for k in pair], 1)
        products = transformed(values)
        for place, k in enumerate(pair):
            cos_part = products[:512, LANES * place : LANES * (place + 1)]
            sin_part = turned(products[512:, LANES * place : LANES * (place + 1)])
            rows = pl.ds(32 * k, 32)
            out_ref[:, 0, rows] = (cos_part + sin_part).reshape(16, 32, LANES)
            mirrored = permuted((cos_part - sin_part) * sign, back)
            edge = extra if k == 0 else pltpu.roll(extra, LANES - k, 1)
            out_ref[:, 1, rows] = jnp.where(lane % 16 == 0, edge, mirrored).reshape(16, 32, LANES)


def signed_freq(counter, length):
    shifted = (counter + length // 2) % length - length // 2
    return shifted.astype(F32) / (length / 2.0)


def x_kernel(data_ref, high_ref, low_ref, solid_hbm, orient_hbm, cross_hbm, solid_ref, orient_ref, cross_ref, first_ref, rest_ref, sems):
    py, pz = lax.axis_index("py"), lax.axis_index("pz")
    flip = (pz >= 8).astype(jnp.int32)
    high, low = high_ref[...], low_ref[...]
    kx = lax.broadcasted_iota(jnp.int32, (32, 256), 1)
    kz = lax.broadcasted_iota(jnp.int32, (32, 256), 0) + pz * 32
    plane = jnp.exp(-0.5 * (signed_freq(kx, 256) ** 2 + signed_freq(kz, 512) ** 2)) * (1.0 / 67108864.0)
    copies = []
    for step in range(32 // STEP_KY):
        for own in range(STEP_KY):
            ky = step * STEP_KY + own
            for half in range(2):
                rows = [data_ref[source, half ^ flip, pl.ds(ky, 8, stride=32), :] for source in range(16)]
                turned = jnp.concatenate(rows, 0).T
                joined = jnp.concatenate([turned[:64], turned[64:]], 1)
                first, rest = split(joined)
                start = own * 128 + half * 64
                first_ref[step % 2, start : start + 64] = first
                rest_ref[step % 2, start : start + 64] = rest
        first, rest = first_ref[step % 2], rest_ref[step % 2]
        products = dot(first, high) + (dot(first, low) + dot(rest, high))
        for own in range(STEP_KY):
            ky = step * STEP_KY + own
            index = jnp.full((1, 256), py * 32 + ky, jnp.int32)
            weight = plane * jnp.exp(-0.5 * signed_freq(index, 512) ** 2)
            weight = jnp.where((kx == 0) & (kz == 0) & (index == 0), 0.0, weight)
            for half in range(2):
                start = own * 128 + half * 64
                cos_part = [products[start + 16 * i : start + 16 * (i + 1), :256] for i in range(4)]
                sin_part = [products[start + 16 * i : start + 16 * (i + 1), 256:] for i in range(4)]
                solid_re = cos_part[0] + sin_part[1]
                solid_im = cos_part[1] - sin_part[0]
                orient_re = cos_part[2] + sin_part[3]
                orient_im = cos_part[3] - sin_part[2]
                scaled = weight[16 * half : 16 * (half + 1)]
                where = pl.ds(16 * half, 16)
                solid_ref[ky, where] = scaled * (solid_re * solid_re + solid_im * solid_im)
                orient_ref[ky, where] = scaled * (orient_re * orient_re + orient_im * orient_im)
                cross_ref[0, ky, where] = scaled * (solid_re * orient_re + solid_im * orient_im)
                cross_ref[1, ky, where] = scaled * (solid_im * orient_re - solid_re * orient_im)
        done = pl.ds(step * STEP_KY, STEP_KY)
        pairs = ((solid_ref.at[done], solid_hbm.at[done]), (orient_ref.at[done], orient_hbm.at[done]), (cross_ref.at[:, done], cross_hbm.at[:, done]))
        for number, (source, target) in enumerate(pairs):
            copy = pltpu.make_async_copy(source, target, sems.at[3 * step + number])
            copy.start()
            copies.append(copy)
    for copy in copies:
        copy.wait()


def whole(shape):
    return pl.BlockSpec(shape, lambda *_: (0,) * len(shape))


IN_VMEM = pl.BlockSpec(memory_space=pltpu.VMEM)
IN_HBM = pl.BlockSpec(memory_space=pltpu.HBM)


def body(solid, orientation):
    params = pltpu.CompilerParams(vmem_limit_bytes=VMEM_LIMIT)
    z_params = pltpu.CompilerParams(vmem_limit_bytes=52 * 1024 * 1024)
    z_high, z_low = z_tables()
    by_y = pl.BlockSpec((16, STEP_Y, 512), lambda i: (0, i, 0))
    field = pl.pallas_call(
        z_kernel,
        grid=(32 // STEP_Y,),
        in_specs=[by_y, by_y, whole(z_high.shape), whole(z_low.shape)],
        out_specs=IN_VMEM,
        out_shape=pltpu.VMEM((16, 272, LANES), F32),
        compiler_params=z_params,
        name="z_transform",
    )(solid, orientation, z_high, z_low)
    field = lax.all_to_all(field, "pz", 0, 0, tiled=True)
    y_high, y_low = y_tables()
    field = pl.pallas_call(
        y_kernel,
        in_specs=[IN_VMEM] * 3,
        out_specs=IN_VMEM,
        out_shape=pltpu.VMEM((16, 2, 256, LANES), F32),
        compiler_params=params,
        name="y_transform",
    )(field, y_high, y_low)
    groups = [[py * 16 + pz for py in range(16) for pz in (low, 15 - low)] for low in range(8)]
    field = lax.all_to_all(
        field.reshape(32, 256, LANES), ("py", "pz"), 0, 0, tiled=True, axis_index_groups=groups
    ).reshape(16, 2, 256, LANES)
    x_high, x_low = x_tables()
    out = jax.ShapeDtypeStruct((32, 32, 256), F32)
    wide = jax.ShapeDtypeStruct((2, 32, 32, 256), F32)
    steps = 32 // STEP_KY
    return tuple(
        pl.pallas_call(
            x_kernel,
            in_specs=[IN_VMEM] * 3,
            out_specs=[IN_HBM] * 3,
            out_shape=[out, out, wide],
            scratch_shapes=[
                pltpu.VMEM(out.shape, F32),
                pltpu.VMEM(out.shape, F32),
                pltpu.VMEM(wide.shape, F32),
                pltpu.VMEM((2, STEP_KY * 128, 256), BF16),
                pltpu.VMEM((2, STEP_KY * 128, 256), BF16),
                pltpu.SemaphoreType.DMA((3 * steps,)),
            ],
            compiler_params=params,
            name="x_transform",
        )(field, x_high, x_low)
    )


def solution(mesh):
    placed = (P("py", "pz", None), P("py", "pz", None))
    return jax.shard_map(
        body,
        mesh=mesh,
        in_specs=placed,
        out_specs=(P("py", "pz", None), P("py", "pz", None), P(None, "py", "pz", None)),
        check_vma=False,
    )
```

time: 170 us -> 163 us (0.959)
  blocking collectives: 35.8 us -> 143 us
  waiting for transfers between devices: 97.5 us -> 0 us
  starting transfers between devices: 10.5 us -> 0 us
  Pallas kernels: 24.2 us -> 18.6 us
    all_to_all x1 -> x2, blocking collectives: 35.8 us -> 143 us  [the longest x1 109 us: body(): lax.all_to_all(field.reshape(32, 256, LANES), ('py', 'pz'), 0, 0, tiled=T...]
    all_to_all x1 -> x0, waiting for transfers between devices: 97.5 us -> none  [body(): lax.all_to_all(field.reshape(32, 8 * 32, LANES), ('py', 'pz'), 0, 0, tile...]
    all_to_all x1 -> x0, starting transfers between devices: 10.5 us -> none  [body(): lax.all_to_all(field.reshape(32, 8 * 32, LANES), ('py', 'pz'), 0, 0, tile...]
    pallas_call x3, Pallas kernels: 24.2 us -> 18.6 us  [the longest x1 7.31 us: body(): pl.pallas_call(x_kernel, in_specs=[IN_VMEM] * 3, out_specs=[IN_HBM] * 3,...]
  transfers between devices with their start and end apart: 1 -> 0, of which waited for: 1 -> 0; matrix products, arithmetic and copies ran while one was open for 0% -> 0% of each run, Pallas kernels for 0% -> 0%
where the time goes in v2:
time: 163 us; the launch traced here: 162 us
  blocking collectives  143 us (88%)
  Pallas kernels  18.6 us (11%)
    all_to_all x1, blocking collectives, body(): lax.all_to_all(field.reshape(32, 256, LANES), ('py', 'pz'), 0, 0, tiled=T...  109 us
    all_to_all x1, blocking collectives, body(): field = lax.all_to_all(field, 'pz', 0, 0, tiled=True)  34 us
    pallas_call x1, Pallas kernels, body(): pl.pallas_call(x_kernel, in_specs=[IN_VMEM] * 3, out_specs=[IN_HBM] * 3,...  7.31 us
    pallas_call x1, Pallas kernels, body(): pl.pallas_call(z_kernel, grid=(32 // STEP_Y,), in_specs=[by_y, by_y, whol...  6.27 us
    pallas_call x1, Pallas kernels, body(): pl.pallas_call(y_kernel, in_specs=[IN_VMEM] * 3, out_specs=IN_VMEM, out_s...  5.02 us

profile of v2, /device:TPU:33, one launch (start us, length us, event | category | flops | bytes accessed | tf_op | source)
XLA Modules:
  0.0 162.4 jit_solution(16099817752131748048)
XLA Ops:
  0.6 6.3 %z_transform.1 = f32[16,272,128]{2,1,0:T(8,128)S(1)} custom-call(s32[16,32,512]{2,1,0:T(8,128)} %solid_ref.1, f32[16,32,512]{2,1,0:T(8,128)} %orient_ref.1, bf16[512,640]{1,0:T(8,128)(2,1)} %constant.12.clone.high_ref, bf16[512,640]{1,0:T(8,128)(2,1)} %constant.13.clone.low_ref), custom_call_target="tpu_custom_call" | custom-call | tf_op jit(solution)/shard_map/z_transform/pallas_call | solution.py:209
  6.9 0.0 copy-start
  6.9 0.0 copy-start.1
  6.9 34.0 %all_to_all.10.data_ref = f32[16,272,128]{2,1,0:T(8,128)S(1)} all-to-all(f32[16,272,128]{2,1,0:T(8,128)S(1)} %z_transform.1), channel_id=1, replica_groups=mesh['py'=16,'pz'=16] {'pz'}, dimensions={0} | all-to-all | bytes 4456448 | tf_op jit(solution)/shard_map/all_to_all | solution.py:218
  40.9 0.0 copy-done
  40.9 0.0 copy-done.1
  40.9 5.0 %y_transform.1 = f32[16,2,256,128]{3,2,1,0:T(8,128)S(1)} custom-call(f32[16,272,128]{2,1,0:T(8,128)S(1)} %all_to_all.10.data_ref, bf16[1024,512]{1,0:T(8,128)(2,1)S(1)} %copy-done.1, bf16[1024,512]{1,0:T(8,128)(2,1)S(1)} %copy-done), custom_call_target="tpu_custom_call" | custom-call | tf_op jit(solution)/shard_map/y_transform/pallas_call | solution.py:220
  45.9 0.0 copy-start.2
  46.0 0.0 copy-start.3
  46.0 109.1 %all_to_all.11 = f32[32,256,128]{2,1,0:T(8,128)S(1)} all-to-all(f32[32,256,128]{2,1,0:T(8,128)S(1)} %bitcast.3), channel_id=1, replica_groups={{0,15,16,31,32,47,48,63,64,79,80,95,96,111,112,127,128,143,144,159,160,..., dimensions={0} | all-to-all | bytes 8388608 | tf_op jit(solution)/shard_map/all_to_all | solution.py:229
  155.1 0.0 copy-done.2
  155.1 0.0 copy-done.3
  155.1 7.3 %x_transform.1 = (f32[32,32,256]{2,1,0:T(8,128)}, f32[32,32,256]{2,1,0:T(8,128)}, f32[2,32,32,256]{3,2,1,0:T(8,128)}) custom-call(f32[16,2,256,128]{3,2,1,0:T(8,128)S(1)} %bitcast.2, bf16[256,512]{1,0:T(8,128)(2,1)S(1)} %copy-done.3, bf16[256,512]{1,0:T(8,128)(2,1)S(1)} %copy-done.2), custom_call_target="tpu_custom_call" | custom-call | tf_op jit(solution)/shard_map/x_transform/pallas_call | solution.py:237
Async XLA Ops:
  6.9 34.0 %copy-start = (bf16[1024,512]{1,0:T(8,128)(2,1)S(1)}, bf16[1024,512]{1,0:T(8,128)(2,1)}, u32[]{:S(2)}) copy-start(bf16[1024,512]{1,0:T(8,128)(2,1)} %constant.15.clone.low_ref) | copy-start | bytes 3145732
  6.9 34.0 %copy-start.1 = (bf16[1024,512]{1,0:T(8,128)(2,1)S(1)}, bf16[1024,512]{1,0:T(8,128)(2,1)}, u32[]{:S(2)}) copy-start(bf16[1024,512]{1,0:T(8,128)(2,1)} %constant.14.clone.high_ref) | copy-start | bytes 3145732
  45.9 109.2 %copy-start.2 = (bf16[256,512]{1,0:T(8,128)(2,1)S(1)}, bf16[256,512]{1,0:T(8,128)(2,1)}, u32[]{:S(2)}) copy-start(bf16[256,512]{1,0:T(8,128)(2,1)} %constant.17.clone.low_ref) | copy-start | bytes 786436
  46.0 109.2 %copy-start.3 = (bf16[256,512]{1,0:T(8,128)(2,1)S(1)}, bf16[256,512]{1,0:T(8,128)(2,1)}, u32[]{:S(2)}) copy-start(bf16[256,512]{1,0:T(8,128)(2,1)} %constant.16.clone.high_ref) | copy-start | bytes 786436

commit v3 on v2

--- a/solution.py
+++ b/solution.py
@@ -10,8 +10,8 @@
 BF16 = jnp.bfloat16
 LANES = 128
 VMEM_LIMIT = 36 * 1024 * 1024
-STEP_Y = 8
-STEP_KY = 8
+STEP_Y = 16
+STEP_KY = 2
 
 
 def two_parts(table):
@@ -35,14 +35,17 @@
     for place in range(16):
         cos, sin = cos_sin(z, first_kz(place) + np.arange(17), 512)
         regular += [cos[:, :16], -sin[:, :16]]
-        extra += [cos[:, 16:], -sin[:, 16:]]
-    return two_parts(np.concatenate(regular + extra * 4, 1))
+        extra.append((cos[:, 16:], -sin[:, 16:]))
+    spread = [pair[part] for part in range(2) for pair in extra]
+    return two_parts(np.concatenate(regular + spread * 4, 1))
 
 
 def y_tables():
-    n = np.arange(512)
-    cos, sin = cos_sin(n, n, 512)
-    return two_parts(np.concatenate([cos, sin], 0))
+    tables = []
+    for parity in range(2):
+        cos, sin = cos_sin(np.arange(256), 2 * np.arange(256) + parity, 512)
+        tables.append(np.concatenate([cos, sin], 0))
+    return two_parts(np.stack(tables))
 
 
 def x_tables():
@@ -84,8 +87,11 @@
     spot = lane_of((size_y, LANES)) % 16
     solid = solid_ref[...].reshape(2 * rows, 512).astype(F32).astype(BF16)
     orient, rest = split(orient_ref[...].reshape(2 * rows, 512))
-    solid_z = dot(solid, high) + dot(solid, low)
-    orient_z = dot(orient, high) + (dot(orient, low) + dot(rest, high))
+    both = jnp.concatenate([solid, orient], 0)
+    small = dot(both, low)
+    large = dot(jnp.concatenate([both, rest], 0), high)
+    solid_z = large[: 2 * rows] + small[: 2 * rows]
+    orient_z = large[2 * rows : 4 * rows] + (small[2 * rows :] + large[4 * rows :])
     pieces = (solid_z[:rows], orient_z[:rows], solid_z[rows:], orient_z[rows:])
     first = pl.multiple_of(i * size_y, 8)
     for tile in range(4):
@@ -98,44 +104,58 @@
     extra = gathered([piece[:, 512:640] for piece in pieces])
     shift = 8 * (2 * i // chunks)
     place_rows = pl.ds(pl.multiple_of(256 + i * size_y % 16, 8), size_y)
+    sixteen = lane_of((size_y, LANES)) // 16 * 16
+    turned = [permuted(extra[k * size_y : (k + 1) * size_y], sixteen + (spot - k) % 16) for k in range(8)]
+    ours = (spot >= shift) & (spot < shift + 8)
     for place in range(16):
-        spread = permuted(extra, group * 32 + 2 * place + lane // 16 % 2)
-        total = jnp.where(shift == 0, 0.0, out_ref[place, place_rows])
-        for k in range(8):
-            total = jnp.where(spot == k + shift, spread[k * size_y : (k + 1) * size_y], total)
-        out_ref[place, place_rows] = total
+        mixed = turned[0]
+        for k in range(1, 8):
+            mixed = jnp.where(spot == (place + k) % 16, turned[k], mixed)
+        mixed = permuted(mixed, sixteen + (spot + (place - shift)) % 16)
+        before = jnp.where(shift == 0, 0.0, out_ref[place, place_rows])
+        out_ref[place, place_rows] = jnp.where(ours, mixed, before)
 
 
 def y_kernel(data_ref, high_ref, low_ref, out_ref):
-    high, low = high_ref[...], low_ref[...]
-    lane = lane_of((512, LANES))
+    lane = lane_of((256, LANES))
     sign = jnp.where(lane // 16 % 2 == 0, 1.0, -1.0).astype(F32)
     swap = lane ^ 16
     back = lane // 16 * 16 + (16 - lane % 16) % 16
 
-    def transformed(values):
+    def transformed(values, parity):
         first, rest = split(values)
+        high, low = high_ref[parity], low_ref[parity]
         return dot(high, first) + (dot(high, rest) + dot(low, first))
 
     def turned(products):
         return permuted(products, swap) * sign
 
-    border = data_ref[:, 256:272]
-    moved = pltpu.roll(border.reshape(256, LANES), LANES - 8, 1).reshape(16, 16, LANES)
-    products = transformed(jnp.concatenate([border, moved], 1).reshape(512, LANES))
-    extra = (products[:512] - turned(products[512:])) * sign
+    def halves(even, odd):
+        cos_even, cos_odd, sin_even, sin_odd = even[:256], odd[:256], even[256:], odd[256:]
+        return (cos_even + cos_odd, sin_even + sin_odd), (cos_even - cos_odd, sin_even - sin_odd)
+
+    def border(parity):
+        rows = data_ref[:, pl.ds(256 + parity, 8, stride=2), :]
+        moved = pltpu.roll(rows.reshape(LANES, LANES), LANES - 8, 1).reshape(16, 8, LANES)
+        return transformed(jnp.concatenate([rows, moved], 1).reshape(256, LANES), parity)
+
+    def pair_of(step, parity):
+        parts = [data_ref[:, pl.ds(32 * k + parity, 16, stride=2), :].reshape(256, LANES) for k in (2 * step, 2 * step + 1)]
+        return transformed(jnp.concatenate(parts, 1), parity)
+
+    extra = [(cos_part - turned(sin_part)) * sign for cos_part, sin_part in halves(border(0), border(1))]
     for step in range(4):
-        pair = (2 * step, 2 * step + 1)
-        values = jnp.concatenate([data_ref[:, 32 * k : 32 * (k + 1)].reshape(512, LANES) for k in pair], 1)
-        products = transformed(values)
-        for place, k in enumerate(pair):
-            cos_part = products[:512, LANES * place : LANES * (place + 1)]
-            sin_part = turned(products[512:, LANES * place : LANES * (place + 1)])
-            rows = pl.ds(32 * k, 32)
-            out_ref[:, 0, rows] = (cos_part + sin_part).reshape(16, 32, LANES)
-            mirrored = permuted((cos_part - sin_part) * sign, back)
-            edge = extra if k == 0 else pltpu.roll(extra, LANES - k, 1)
-            out_ref[:, 1, rows] = jnp.where(lane % 16 == 0, edge, mirrored).reshape(16, 32, LANES)
+        both = halves(pair_of(step, 0), pair_of(step, 1))
+        for half in range(2):
+            for place in range(2):
+                k = 2 * step + place
+                cos_part, sin_part = [part[:, LANES * place : LANES * (place + 1)] for part in both[half]]
+                sin_part = turned(sin_part)
+                targets, rows = pl.ds(8 * half, 8), pl.ds(32 * k, 32)
+                out_ref[targets, 0, rows] = (cos_part + sin_part).reshape(8, 32, LANES)
+                mirrored = permuted((cos_part - sin_part) * sign, back)
+                edge = extra[half] if k == 0 else pltpu.roll(extra[half], LANES - k, 1)
+                out_ref[targets, 1, rows] = jnp.where(lane % 16 == 0, edge, mirrored).reshape(8, 32, LANES)
 
 
 def signed_freq(counter, length):

time: 163 us -> 158 us (0.969)
  Pallas kernels: 18.6 us -> 13.8 us
    pallas_call x1, Pallas kernels: 5.02 us -> 2.64 us  [body(): pl.pallas_call(y_kernel, in_specs=[IN_VMEM] * 3, out_specs=IN_VMEM, out_s...]
where the time goes in v3:
time: 158 us
  blocking collectives  143 us (91%)
  Pallas kernels  13.8 us (9%)
    all_to_all x1, blocking collectives, body(): lax.all_to_all(field.reshape(32, 256, LANES), ('py', 'pz'), 0, 0, tiled=T...  109 us
    all_to_all x1, blocking collectives, body(): field = lax.all_to_all(field, 'pz', 0, 0, tiled=True)  34 us
    pallas_call x1, Pallas kernels, body(): pl.pallas_call(x_kernel, in_specs=[IN_VMEM] * 3, out_specs=[IN_HBM] * 3,...  6.17 us
    pallas_call x1, Pallas kernels, body(): pl.pallas_call(z_kernel, grid=(32 // STEP_Y,), in_specs=[by_y, by_y, whol...  4.98 us

profile of v3, /device:TPU:33, one launch (start us, length us, event | category | flops | bytes accessed | tf_op | source)
XLA Modules:
  0.0 157.6 jit_solution(550765405542401837)
XLA Ops:
  0.6 5.0 %z_transform.1 = f32[16,272,128]{2,1,0:T(8,128)S(1)} custom-call(s32[16,32,512]{2,1,0:T(8,128)} %solid_ref.1, f32[16,32,512]{2,1,0:T(8,128)} %orient_ref.1, bf16[512,640]{1,0:T(8,128)(2,1)} %constant.12.clone.high_ref, bf16[512,640]{1,0:T(8,128)(2,1)} %constant.13.clone.low_ref), custom_call_target="tpu_custom_call" | custom-call | tf_op jit(solution)/shard_map/z_transform/pallas_call | solution.py:229
  5.6 0.0 copy-start
  5.6 0.0 copy-start.1
  5.6 34.0 %all_to_all.10.data_ref = f32[16,272,128]{2,1,0:T(8,128)S(1)} all-to-all(f32[16,272,128]{2,1,0:T(8,128)S(1)} %z_transform.1), channel_id=1, replica_groups=mesh['py'=16,'pz'=16] {'pz'}, dimensions={0} | all-to-all | bytes 4456448 | tf_op jit(solution)/shard_map/all_to_all | solution.py:238
  39.6 0.0 copy-done
  39.6 0.0 copy-done.1
  39.6 2.6 %y_transform.1 = f32[16,2,256,128]{3,2,1,0:T(8,128)S(1)} custom-call(f32[16,272,128]{2,1,0:T(8,128)S(1)} %all_to_all.10.data_ref, bf16[2,512,256]{2,1,0:T(8,128)(2,1)S(1)} %copy-done.1, bf16[2,512,256]{2,1,0:T(8,128)(2,1)S(1)} %copy-done), custom_call_target="tpu_custom_call" | custom-call | tf_op jit(solution)/shard_map/y_transform/pallas_call | solution.py:240
  42.3 0.0 copy-start.2
  42.3 0.0 copy-start.3
  42.3 109.1 %all_to_all.11 = f32[32,256,128]{2,1,0:T(8,128)S(1)} all-to-all(f32[32,256,128]{2,1,0:T(8,128)S(1)} %bitcast.2), channel_id=1, replica_groups={{0,15,16,31,32,47,48,63,64,79,80,95,96,111,112,127,128,143,144,159,160,..., dimensions={0} | all-to-all | bytes 8388608 | tf_op jit(solution)/shard_map/all_to_all | solution.py:249
  151.4 0.0 copy-done.2
  151.4 0.0 copy-done.3
  151.4 6.2 %x_transform.1 = (f32[32,32,256]{2,1,0:T(8,128)}, f32[32,32,256]{2,1,0:T(8,128)}, f32[2,32,32,256]{3,2,1,0:T(8,128)}) custom-call(f32[16,2,256,128]{3,2,1,0:T(8,128)S(1)} %bitcast.3, bf16[256,512]{1,0:T(8,128)(2,1)S(1)} %copy-done.3, bf16[256,512]{1,0:T(8,128)(2,1)S(1)} %copy-done.2), custom_call_target="tpu_custom_call" | custom-call | tf_op jit(solution)/shard_map/x_transform/pallas_call | solution.py:257
Async XLA Ops:
  5.6 34.0 %copy-start = (bf16[2,512,256]{2,1,0:T(8,128)(2,1)S(1)}, bf16[2,512,256]{2,1,0:T(8,128)(2,1)}, u32[]{:S(2)}) copy-start(bf16[2,512,256]{2,1,0:T(8,128)(2,1)} %constant.15.clone.low_ref) | copy-start | bytes 1572868
  5.6 34.0 %copy-start.1 = (bf16[2,512,256]{2,1,0:T(8,128)(2,1)S(1)}, bf16[2,512,256]{2,1,0:T(8,128)(2,1)}, u32[]{:S(2)}) copy-start(bf16[2,512,256]{2,1,0:T(8,128)(2,1)} %constant.14.clone.high_ref) | copy-start | bytes 1572868
  42.3 109.2 %copy-start.2 = (bf16[256,512]{1,0:T(8,128)(2,1)S(1)}, bf16[256,512]{1,0:T(8,128)(2,1)}, u32[]{:S(2)}) copy-start(bf16[256,512]{1,0:T(8,128)(2,1)} %constant.17.clone.low_ref) | copy-start | bytes 786436
  42.3 109.2 %copy-start.3 = (bf16[256,512]{1,0:T(8,128)(2,1)S(1)}, bf16[256,512]{1,0:T(8,128)(2,1)}, u32[]{:S(2)}) copy-start(bf16[256,512]{1,0:T(8,128)(2,1)} %constant.16.clone.high_ref) | copy-start | bytes 786436

commit v4 on v3

--- a/solution.py
+++ b/solution.py
@@ -11,7 +11,7 @@
 LANES = 128
 VMEM_LIMIT = 36 * 1024 * 1024
 STEP_Y = 16
-STEP_KY = 2
+STEP_KY = 4
 
 
 def two_parts(table):
@@ -51,8 +51,8 @@
 def x_tables():
     half, source, low = np.meshgrid(np.arange(2), np.arange(16), np.arange(8), indexing="ij")
     x = (source * 16 + half * 8 + low).reshape(-1)
-    cos, sin = cos_sin(x, np.arange(256), 256)
-    return two_parts(np.concatenate([cos, sin], 1))
+    cos, sin = cos_sin(x, np.arange(129), 256)
+    return two_parts(np.concatenate([cos[:, :128], cos[:, 128:], sin[:, 1:128]], 1))
 
 
 def split(values):
@@ -151,11 +151,11 @@
                 k = 2 * step + place
                 cos_part, sin_part = [part[:, LANES * place : LANES * (place + 1)] for part in both[half]]
                 sin_part = turned(sin_part)
-                targets, rows = pl.ds(8 * half, 8), pl.ds(32 * k, 32)
-                out_ref[targets, 0, rows] = (cos_part + sin_part).reshape(8, 32, LANES)
+                targets = pl.ds(8 * half, 8)
+                out_ref[targets, 0, :, k] = (cos_part + sin_part).reshape(8, 4, 8, LANES)
                 mirrored = permuted((cos_part - sin_part) * sign, back)
                 edge = extra[half] if k == 0 else pltpu.roll(extra[half], LANES - k, 1)
-                out_ref[targets, 1, rows] = jnp.where(lane % 16 == 0, edge, mirrored).reshape(8, 32, LANES)
+                out_ref[targets, 1, :, k] = jnp.where(lane % 16 == 0, edge, mirrored).reshape(8, 4, 8, LANES)
 
 
 def signed_freq(counter, length):
@@ -167,15 +167,23 @@
     py, pz = lax.axis_index("py"), lax.axis_index("pz")
     flip = (pz >= 8).astype(jnp.int32)
     high, low = high_ref[...], low_ref[...]
-    kx = lax.broadcasted_iota(jnp.int32, (32, 256), 1)
-    kz = lax.broadcasted_iota(jnp.int32, (32, 256), 0) + pz * 32
-    plane = jnp.exp(-0.5 * (signed_freq(kx, 256) ** 2 + signed_freq(kz, 512) ** 2)) * (1.0 / 67108864.0)
+    lane = lane_of((16, LANES))
+    edge = lane == 0
+    back = (LANES - lane) % LANES
+    kx = lane_of((32, LANES))
+    kz = lax.broadcasted_iota(jnp.int32, (32, LANES), 0) + pz * 32
+    freq_z = signed_freq(kz, 512) ** 2
+    planes = [
+        jnp.exp(-0.5 * (signed_freq(k, 256) ** 2 + freq_z)) * (1.0 / 67108864.0)
+        for k in (kx, jnp.where(kx == 0, 128, kx))
+    ]
+    origin = (kx == 0) & (kz == 0)
     copies = []
     for step in range(32 // STEP_KY):
         for own in range(STEP_KY):
             ky = step * STEP_KY + own
             for half in range(2):
-                rows = [data_ref[source, half ^ flip, pl.ds(ky, 8, stride=32), :] for source in range(16)]
+                rows = [data_ref[source, half ^ flip, pl.ds(ky // 8 * 64 + ky % 8, 8, stride=8), :] for source in range(16)]
                 turned = jnp.concatenate(rows, 0).T
                 joined = jnp.concatenate([turned[:64], turned[64:]], 1)
                 first, rest = split(joined)
@@ -186,23 +194,40 @@
         products = dot(first, high) + (dot(first, low) + dot(rest, high))
         for own in range(STEP_KY):
             ky = step * STEP_KY + own
-            index = jnp.full((1, 256), py * 32 + ky, jnp.int32)
-            weight = plane * jnp.exp(-0.5 * signed_freq(index, 512) ** 2)
-            weight = jnp.where((kx == 0) & (kz == 0) & (index == 0), 0.0, weight)
+            index = jnp.full((1, LANES), py * 32 + ky, jnp.int32)
+            own_weight = jnp.exp(-0.5 * signed_freq(index, 512) ** 2)
+            weights = (jnp.where(origin & (index == 0), 0.0, planes[0] * own_weight), planes[1] * own_weight)
             for half in range(2):
                 start = own * 128 + half * 64
-                cos_part = [products[start + 16 * i : start + 16 * (i + 1), :256] for i in range(4)]
-                sin_part = [products[start + 16 * i : start + 16 * (i + 1), 256:] for i in range(4)]
-                solid_re = cos_part[0] + sin_part[1]
-                solid_im = cos_part[1] - sin_part[0]
-                orient_re = cos_part[2] + sin_part[3]
-                orient_im = cos_part[3] - sin_part[2]
-                scaled = weight[16 * half : 16 * (half + 1)]
+                cos_part = [products[start + 16 * i : start + 16 * (i + 1), :LANES] for i in range(4)]
+                sin_part = [products[start + 16 * i : start + 16 * (i + 1), LANES:] for i in range(4)]
+                sin_only = [jnp.where(edge, 0.0, part) for part in sin_part]
                 where = pl.ds(16 * half, 16)
-                solid_ref[ky, where] = scaled * (solid_re * solid_re + solid_im * solid_im)
-                orient_ref[ky, where] = scaled * (orient_re * orient_re + orient_im * orient_im)
-                cross_ref[0, ky, where] = scaled * (solid_re * orient_re + solid_im * orient_im)
-                cross_ref[1, ky, where] = scaled * (solid_im * orient_re - solid_re * orient_im)
+                for side in range(2):
+                    fields = []
+                    for re, im in ((0, 1), (2, 3)):
+                        if side == 0:
+                            fields += [cos_part[re] + sin_only[im], cos_part[im] - sin_only[re]]
+                        else:
+                            fields += [
+                                jnp.where(edge, sin_part[re], cos_part[re] - sin_part[im]),
+                                jnp.where(edge, sin_part[im], cos_part[im] + sin_part[re]),
+                            ]
+                    solid_re, solid_im, orient_re, orient_im = fields
+                    scaled = weights[side][16 * half : 16 * (half + 1)]
+                    results = [
+                        scaled * (solid_re * solid_re + solid_im * solid_im),
+                        scaled * (orient_re * orient_re + orient_im * orient_im),
+                        scaled * (solid_re * orient_re + solid_im * orient_im),
+                        scaled * (solid_im * orient_re - solid_re * orient_im),
+                    ]
+                    if side == 1:
+                        results = [permuted(result, back) for result in results]
+                    there = pl.ds(LANES * side, LANES)
+                    solid_ref[ky, where, there] = results[0]
+                    orient_ref[ky, where, there] = results[1]
+                    cross_ref[0, ky, where, there] = results[2]
+                    cross_ref[1, ky, where, there] = results[3]
         done = pl.ds(step * STEP_KY, STEP_KY)
         pairs = ((solid_ref.at[done], solid_hbm.at[done]), (orient_ref.at[done], orient_hbm.at[done]), (cross_ref.at[:, done], cross_hbm.at[:, done]))
         for number, (source, target) in enumerate(pairs):
@@ -241,7 +266,7 @@
         y_kernel,
         in_specs=[IN_VMEM] * 3,
         out_specs=IN_VMEM,
-        out_shape=pltpu.VMEM((16, 2, 256, LANES), F32),
+        out_shape=pltpu.VMEM((16, 2, 4, 8, 8, LANES), F32),
         compiler_params=params,
         name="y_transform",
     )(field, y_high, y_low)

time: 158 us -> 156 us (0.987)
  Pallas kernels: 13.8 us -> 11.5 us
    pallas_call x1, Pallas kernels: 6.17 us -> 3.89 us  [body(): pl.pallas_call(x_kernel, in_specs=[IN_VMEM] * 3, out_specs=[IN_HBM] * 3,...]
where the time goes in v4:
time: 156 us; the launch traced here: 155 us
  blocking collectives  143 us (92%)
  Pallas kernels  11.5 us (7%)
    all_to_all x1, blocking collectives, body(): lax.all_to_all(field.reshape(32, 256, LANES), ('py', 'pz'), 0, 0, tiled=T...  109 us
    all_to_all x1, blocking collectives, body(): field = lax.all_to_all(field, 'pz', 0, 0, tiled=True)  34 us
    pallas_call x1, Pallas kernels, body(): pl.pallas_call(z_kernel, grid=(32 // STEP_Y,), in_specs=[by_y, by_y, whol...  4.98 us
    pallas_call x1, Pallas kernels, body(): pl.pallas_call(x_kernel, in_specs=[IN_VMEM] * 3, out_specs=[IN_HBM] * 3,...  3.89 us

profile of v4, /device:TPU:33, one launch (start us, length us, event | category | flops | bytes accessed | tf_op | source)
XLA Modules:
  0.0 155.3 jit_solution(5506984407817784150)
XLA Ops:
  0.6 5.0 %z_transform.1 = f32[16,272,128]{2,1,0:T(8,128)S(1)} custom-call(s32[16,32,512]{2,1,0:T(8,128)} %solid_ref.1, f32[16,32,512]{2,1,0:T(8,128)} %orient_ref.1, bf16[512,640]{1,0:T(8,128)(2,1)} %constant.12.clone.high_ref, bf16[512,640]{1,0:T(8,128)(2,1)} %constant.13.clone.low_ref), custom_call_target="tpu_custom_call" | custom-call | tf_op jit(solution)/shard_map/z_transform/pallas_call | solution.py:254
  5.6 0.0 copy-start
  5.6 0.0 copy-start.1
  5.6 34.0 %all_to_all.10.data_ref = f32[16,272,128]{2,1,0:T(8,128)S(1)} all-to-all(f32[16,272,128]{2,1,0:T(8,128)S(1)} %z_transform.1), channel_id=1, replica_groups=mesh['py'=16,'pz'=16] {'pz'}, dimensions={0} | all-to-all | bytes 4456448 | tf_op jit(solution)/shard_map/all_to_all | solution.py:263
  39.6 0.0 copy-done
  39.6 0.0 copy-done.1
  39.6 2.6 %y_transform.1 = f32[16,2,4,8,8,128]{5,4,3,2,1,0:T(8,128)S(1)} custom-call(f32[16,272,128]{2,1,0:T(8,128)S(1)} %all_to_all.10.data_ref, bf16[2,512,256]{2,1,0:T(8,128)(2,1)S(1)} %copy-done.1, bf16[2,512,256]{2,1,0:T(8,128)(2,1)S(1)} %copy-done), custom_call_target="tpu_custom_call" | custom-call | tf_op jit(solution)/shard_map/y_transform/pallas_call | solution.py:265
  42.3 0.0 copy-start.2
  42.3 0.0 copy-start.3
  42.3 109.1 %all_to_all.11 = f32[32,256,128]{2,1,0:T(8,128)S(1)} all-to-all(f32[32,256,128]{2,1,0:T(8,128)S(1)} %bitcast.2), channel_id=1, replica_groups={{0,15,16,31,32,47,48,63,64,79,80,95,96,111,112,127,128,143,144,159,160,..., dimensions={0} | all-to-all | bytes 8388608 | tf_op jit(solution)/shard_map/all_to_all | solution.py:274
  151.4 0.0 copy-done.2
  151.4 0.0 copy-done.3
  151.4 3.9 %x_transform.1 = (f32[32,32,256]{2,1,0:T(8,128)}, f32[32,32,256]{2,1,0:T(8,128)}, f32[2,32,32,256]{3,2,1,0:T(8,128)}) custom-call(f32[16,2,256,128]{3,2,1,0:T(8,128)S(1)} %bitcast.3, bf16[256,256]{1,0:T(8,128)(2,1)S(1)} %copy-done.3, bf16[256,256]{1,0:T(8,128)(2,1)S(1)} %copy-done.2), custom_call_target="tpu_custom_call" | custom-call | tf_op jit(solution)/shard_map/x_transform/pallas_call | solution.py:282
Async XLA Ops:
  5.6 34.0 %copy-start = (bf16[2,512,256]{2,1,0:T(8,128)(2,1)S(1)}, bf16[2,512,256]{2,1,0:T(8,128)(2,1)}, u32[]{:S(2)}) copy-start(bf16[2,512,256]{2,1,0:T(8,128)(2,1)} %constant.15.clone.low_ref) | copy-start | bytes 1572868
  5.6 34.0 %copy-start.1 = (bf16[2,512,256]{2,1,0:T(8,128)(2,1)S(1)}, bf16[2,512,256]{2,1,0:T(8,128)(2,1)}, u32[]{:S(2)}) copy-start(bf16[2,512,256]{2,1,0:T(8,128)(2,1)} %constant.14.clone.high_ref) | copy-start | bytes 1572868
  42.3 109.2 %copy-start.2 = (bf16[256,256]{1,0:T(8,128)(2,1)S(1)}, bf16[256,256]{1,0:T(8,128)(2,1)}, u32[]{:S(2)}) copy-start(bf16[256,256]{1,0:T(8,128)(2,1)} %constant.17.clone.low_ref) | copy-start | bytes 393220
  42.3 109.2 %copy-start.3 = (bf16[256,256]{1,0:T(8,128)(2,1)S(1)}, bf16[256,256]{1,0:T(8,128)(2,1)}, u32[]{:S(2)}) copy-start(bf16[256,256]{1,0:T(8,128)(2,1)} %constant.16.clone.high_ref) | copy-start | bytes 393220

commit v5 on v4

--- a/solution.py
+++ b/solution.py
@@ -30,14 +30,15 @@
 
 
 def z_tables():
-    z = np.arange(512)
-    regular, extra = [], []
-    for place in range(16):
-        cos, sin = cos_sin(z, first_kz(place) + np.arange(17), 512)
-        regular += [cos[:, :16], -sin[:, :16]]
-        extra.append((cos[:, 16:], -sin[:, 16:]))
-    spread = [pair[part] for part in range(2) for pair in extra]
-    return two_parts(np.concatenate(regular + spread * 4, 1))
+    z = np.arange(256)
+    none = np.zeros((256, 256))
+    parts = [cos_sin(z, first_kz(place) + np.arange(17), 512) for place in range(16)]
+    cos = np.concatenate([part[0][:, :16] for part in parts], 1)
+    sin = np.concatenate([part[1][:, :16] for part in parts], 1)
+    last_cos = np.concatenate([part[0][:, 16:] for part in parts] + [none[:, :16]], 1)
+    last_sin = np.concatenate([none[:, :16]] + [-part[1][:, 16:] for part in parts], 1)
+    even, odd = np.concatenate([cos] + [last_cos] * 4, 1), np.concatenate([-sin] + [last_sin] * 4, 1)
+    return two_parts(np.stack([even, odd]))
 
 
 def y_tables():
@@ -77,31 +78,54 @@
     rows = 8 * size_y
     chunks = 32 // size_y
     i = pl.program_id(0)
-    high, low = high_ref[...], low_ref[...]
     lane = lane_of((rows, LANES))
     group = lane // 32
+    row_lane = lane_of((2 * rows, LANES))
+    edge = row_lane == 0
+    back = (LANES - row_lane) % LANES
 
     def gathered(items):
         return jnp.where(group == 0, items[0], jnp.where(group == 1, items[1], jnp.where(group == 2, items[2], items[3])))
 
+    def folded(values):
+        parts = [values[:, LANES * n : LANES * (n + 1)] for n in range(4)]
+        far, near = permuted(parts[3], back), permuted(parts[2], back)
+        facing = jnp.concatenate([jnp.where(edge, 0.0, far), jnp.where(edge, far, near)], 1)
+        return values[:, :256] + facing, values[:, :256] - facing, near[:, :1]
+
+    *solids, solid_mid = folded(solid_ref[...].reshape(2 * rows, 512).astype(F32))
+    *orients, orient_mid = folded(orient_ref[...].reshape(2 * rows, 512))
+    solid_z, orient_z = [], []
+    for part in range(2):
+        orient, rest = split(orients[part])
+        both = jnp.concatenate([solids[part].astype(BF16), orient], 0)
+        small = dot(both, low_ref[part])
+        large = dot(jnp.concatenate([both, rest], 0), high_ref[part])
+        solid_z.append(large[: 2 * rows] + small[: 2 * rows])
+        orient_z.append(large[2 * rows : 4 * rows] + (small[2 * rows :] + large[4 * rows :]))
+    wide = lane_of((2 * rows, 384))
+    share = jnp.where(wide < 256, jnp.where(wide % 2 == 0, 1.0, -1.0), jnp.where(wide // 16 % 2 == 0, 1.0, 0.0))
+    solid_z[0] += solid_mid * share
+    orient_z[0] += orient_mid * share
     spot = lane_of((size_y, LANES)) % 16
-    solid = solid_ref[...].reshape(2 * rows, 512).astype(F32).astype(BF16)
-    orient, rest = split(orient_ref[...].reshape(2 * rows, 512))
-    both = jnp.concatenate([solid, orient], 0)
-    small = dot(both, low)
-    large = dot(jnp.concatenate([both, rest], 0), high)
-    solid_z = large[: 2 * rows] + small[: 2 * rows]
-    orient_z = large[2 * rows : 4 * rows] + (small[2 * rows :] + large[4 * rows :])
-    pieces = (solid_z[:rows], orient_z[:rows], solid_z[rows:], orient_z[rows:])
+    halves = (slice(0, rows), slice(rows, 2 * rows))
     first = pl.multiple_of(i * size_y, 8)
-    for tile in range(4):
-        columns = [piece[:, LANES * tile : LANES * (tile + 1)] for piece in pieces]
-        for q in range(4):
-            moved = [columns[c] if c == q else pltpu.roll(columns[c], 32 * (c - q) % LANES, 1) for c in range(4)]
-            ready = gathered(moved)
+    for tile in range(2):
+        columns = slice(LANES * tile, LANES * (tile + 1))
+        blocks = [field[part][half, columns] for half in halves for field in (solid_z, orient_z) for part in range(2)]
+        for bit in (1, 2, 4):
+            unset = lane // 16 // bit % 2 == 0
+            for c in range(8):
+                if c & bit == 0:
+                    one, two = blocks[c], blocks[c | bit]
+                    moving = jnp.where(unset, two, one)
+                    moved = pltpu.roll(moving, 64, 1) if bit == 4 else permuted(moving, lane ^ 16 * bit)
+                    blocks[c] = jnp.where(unset, one, moved)
+                    blocks[c | bit] = jnp.where(unset, moved, two)
+        for q in range(8):
             for k in range(8):
-                out_ref[4 * tile + q, pl.ds(32 * k + first, size_y)] = ready[k * size_y : (k + 1) * size_y]
-    extra = gathered([piece[:, 512:640] for piece in pieces])
+                out_ref[8 * tile + q, pl.ds(32 * k + first, size_y)] = blocks[q][k * size_y : (k + 1) * size_y]
+    extra = gathered([field[0][half, 256:] + field[1][half, 256:] for half in halves for field in (solid_z, orient_z)])
     shift = 8 * (2 * i // chunks)
     place_rows = pl.ds(pl.multiple_of(256 + i * size_y % 16, 8), size_y)
     sixteen = lane_of((size_y, LANES)) // 16 * 16

time: 156 us -> 155 us (level)
  no operation moved by 1% of the time
where the time goes in v5:
time: 155 us
  blocking collectives  143 us (92%)
  Pallas kernels  10.9 us (7%)
    all_to_all x1, blocking collectives, body(): lax.all_to_all(field.reshape(32, 256, LANES), ('py', 'pz'), 0, 0, tiled=T...  109 us
    all_to_all x1, blocking collectives, body(): field = lax.all_to_all(field, 'pz', 0, 0, tiled=True)  34 us
    pallas_call x1, Pallas kernels, body(): pl.pallas_call(z_kernel, grid=(32 // STEP_Y,), in_specs=[by_y, by_y, whol...  4.38 us
    pallas_call x1, Pallas kernels, body(): pl.pallas_call(x_kernel, in_specs=[IN_VMEM] * 3, out_specs=[IN_HBM] * 3,...  3.9 us

profile of v5, /device:TPU:33, one launch (start us, length us, event | category | flops | bytes accessed | tf_op | source)
XLA Modules:
  0.0 154.8 jit_solution(17945311915405400839)
XLA Ops:
  0.6 4.4 %z_transform.1 = f32[16,272,128]{2,1,0:T(8,128)S(1)} custom-call(s32[16,32,512]{2,1,0:T(8,128)} %solid_ref.1, f32[16,32,512]{2,1,0:T(8,128)} %orient_ref.1, bf16[2,256,384]{2,1,0:T(8,128)(2,1)} %constant.12.clone.high_ref, bf16[2,256,384]{2,1,0:T(8,128)(2,1)} %constant.13.clone.low_ref), custom_call_target="tpu_custom_call" | custom-call | tf_op jit(solution)/shard_map/z_transform/pallas_call | solution.py:278
  5.0 0.0 copy-start
  5.0 0.0 copy-start.1
  5.0 34.0 %all_to_all.10.data_ref = f32[16,272,128]{2,1,0:T(8,128)S(1)} all-to-all(f32[16,272,128]{2,1,0:T(8,128)S(1)} %z_transform.1), channel_id=1, replica_groups=mesh['py'=16,'pz'=16] {'pz'}, dimensions={0} | all-to-all | bytes 4456448 | tf_op jit(solution)/shard_map/all_to_all | solution.py:287
  39.0 0.0 copy-done
  39.0 0.0 copy-done.1
  39.0 2.6 %y_transform.1 = f32[16,2,4,8,8,128]{5,4,3,2,1,0:T(8,128)S(1)} custom-call(f32[16,272,128]{2,1,0:T(8,128)S(1)} %all_to_all.10.data_ref, bf16[2,512,256]{2,1,0:T(8,128)(2,1)S(1)} %copy-done.1, bf16[2,512,256]{2,1,0:T(8,128)(2,1)S(1)} %copy-done), custom_call_target="tpu_custom_call" | custom-call | tf_op jit(solution)/shard_map/y_transform/pallas_call | solution.py:289
  41.7 0.0 copy-start.2
  41.7 0.0 copy-start.3
  41.7 109.2 %all_to_all.11 = f32[32,256,128]{2,1,0:T(8,128)S(1)} all-to-all(f32[32,256,128]{2,1,0:T(8,128)S(1)} %bitcast.2), channel_id=1, replica_groups={{0,15,16,31,32,47,48,63,64,79,80,95,96,111,112,127,128,143,144,159,160,..., dimensions={0} | all-to-all | bytes 8388608 | tf_op jit(solution)/shard_map/all_to_all | solution.py:298
  150.9 0.0 copy-done.2
  150.9 0.0 copy-done.3
  150.9 3.9 %x_transform.1 = (f32[32,32,256]{2,1,0:T(8,128)}, f32[32,32,256]{2,1,0:T(8,128)}, f32[2,32,32,256]{3,2,1,0:T(8,128)}) custom-call(f32[16,2,256,128]{3,2,1,0:T(8,128)S(1)} %bitcast.3, bf16[256,256]{1,0:T(8,128)(2,1)S(1)} %copy-done.3, bf16[256,256]{1,0:T(8,128)(2,1)S(1)} %copy-done.2), custom_call_target="tpu_custom_call" | custom-call | tf_op jit(solution)/shard_map/x_transform/pallas_call | solution.py:306
Async XLA Ops:
  5.0 34.0 %copy-start = (bf16[2,512,256]{2,1,0:T(8,128)(2,1)S(1)}, bf16[2,512,256]{2,1,0:T(8,128)(2,1)}, u32[]{:S(2)}) copy-start(bf16[2,512,256]{2,1,0:T(8,128)(2,1)} %constant.15.clone.low_ref) | copy-start | bytes 1572868
  5.0 34.0 %copy-start.1 = (bf16[2,512,256]{2,1,0:T(8,128)(2,1)S(1)}, bf16[2,512,256]{2,1,0:T(8,128)(2,1)}, u32[]{:S(2)}) copy-start(bf16[2,512,256]{2,1,0:T(8,128)(2,1)} %constant.14.clone.high_ref) | copy-start | bytes 1572868
  41.7 109.2 %copy-start.2 = (bf16[256,256]{1,0:T(8,128)(2,1)S(1)}, bf16[256,256]{1,0:T(8,128)(2,1)}, u32[]{:S(2)}) copy-start(bf16[256,256]{1,0:T(8,128)(2,1)} %constant.17.clone.low_ref) | copy-start | bytes 393220
  41.7 109.2 %copy-start.3 = (bf16[256,256]{1,0:T(8,128)(2,1)S(1)}, bf16[256,256]{1,0:T(8,128)(2,1)}, u32[]{:S(2)}) copy-start(bf16[256,256]{1,0:T(8,128)(2,1)} %constant.16.clone.high_ref) | copy-start | bytes 393220

commit v6 on v5

--- a/solution.py
+++ b/solution.py
@@ -176,10 +176,10 @@
                 cos_part, sin_part = [part[:, LANES * place : LANES * (place + 1)] for part in both[half]]
                 sin_part = turned(sin_part)
                 targets = pl.ds(8 * half, 8)
-                out_ref[targets, 0, :, k] = (cos_part + sin_part).reshape(8, 4, 8, LANES)
+                out_ref[0, targets, :, k] = (cos_part + sin_part).reshape(8, 4, 8, LANES)
                 mirrored = permuted((cos_part - sin_part) * sign, back)
                 edge = extra[half] if k == 0 else pltpu.roll(extra[half], LANES - k, 1)
-                out_ref[targets, 1, :, k] = jnp.where(lane % 16 == 0, edge, mirrored).reshape(8, 4, 8, LANES)
+                out_ref[1, targets, :, k] = jnp.where(lane % 16 == 0, edge, mirrored).reshape(8, 4, 8, LANES)
 
 
 def signed_freq(counter, length):
@@ -207,7 +207,7 @@
         for own in range(STEP_KY):
             ky = step * STEP_KY + own
             for half in range(2):
-                rows = [data_ref[source, half ^ flip, pl.ds(ky // 8 * 64 + ky % 8, 8, stride=8), :] for source in range(16)]
+                rows = [data_ref[half ^ flip, source, pl.ds(ky // 8 * 64 + ky % 8, 8, stride=8), :] for source in range(16)]
                 turned = jnp.concatenate(rows, 0).T
                 joined = jnp.concatenate([turned[:64], turned[64:]], 1)
                 first, rest = split(joined)
@@ -290,14 +290,14 @@
         y_kernel,
         in_specs=[IN_VMEM] * 3,
         out_specs=IN_VMEM,
-        out_shape=pltpu.VMEM((16, 2, 4, 8, 8, LANES), F32),
+        out_shape=pltpu.VMEM((2, 16, 4, 8, 8, LANES), F32),
         compiler_params=params,
         name="y_transform",
     )(field, y_high, y_low)
-    groups = [[py * 16 + pz for py in range(16) for pz in (low, 15 - low)] for low in range(8)]
+    groups = [[py * 16 + pz for pz in (low, 15 - low) for py in range(16)] for low in range(8)]
     field = lax.all_to_all(
         field.reshape(32, 256, LANES), ("py", "pz"), 0, 0, tiled=True, axis_index_groups=groups
-    ).reshape(16, 2, 256, LANES)
+    ).reshape(2, 16, 256, LANES)
     x_high, x_low = x_tables()
     out = jax.ShapeDtypeStruct((32, 32, 256), F32)
     wide = jax.ShapeDtypeStruct((2, 32, 32, 256), F32)

time: 155 us -> 155 us (level)
  no operation moved by 1% of the time
where the time goes in v6:
time: 155 us; the launch traced here: 154 us
  blocking collectives  142 us (92%)
  Pallas kernels  10.9 us (7%)
    all_to_all x1, blocking collectives, body(): lax.all_to_all(field.reshape(32, 256, LANES), ('py', 'pz'), 0, 0, tiled=T...  108 us
    all_to_all x1, blocking collectives, body(): field = lax.all_to_all(field, 'pz', 0, 0, tiled=True)  34 us
    pallas_call x1, Pallas kernels, body(): pl.pallas_call(z_kernel, grid=(32 // STEP_Y,), in_specs=[by_y, by_y, whol...  4.38 us
    pallas_call x1, Pallas kernels, body(): pl.pallas_call(x_kernel, in_specs=[IN_VMEM] * 3, out_specs=[IN_HBM] * 3,...  3.89 us

profile of v6, /device:TPU:33, one launch (start us, length us, event | category | flops | bytes accessed | tf_op | source)
XLA Modules:
  0.0 153.8 jit_solution(14407181912060154248)
XLA Ops:
  0.6 4.4 %z_transform.1 = f32[16,272,128]{2,1,0:T(8,128)S(1)} custom-call(s32[16,32,512]{2,1,0:T(8,128)} %solid_ref.1, f32[16,32,512]{2,1,0:T(8,128)} %orient_ref.1, bf16[2,256,384]{2,1,0:T(8,128)(2,1)} %constant.12.clone.high_ref, bf16[2,256,384]{2,1,0:T(8,128)(2,1)} %constant.13.clone.low_ref), custom_call_target="tpu_custom_call" | custom-call | tf_op jit(solution)/shard_map/z_transform/pallas_call | solution.py:278
  5.0 0.0 copy-start
  5.0 0.0 copy-start.1
  5.0 34.0 %all_to_all.10.data_ref = f32[16,272,128]{2,1,0:T(8,128)S(1)} all-to-all(f32[16,272,128]{2,1,0:T(8,128)S(1)} %z_transform.1), channel_id=1, replica_groups=mesh['py'=16,'pz'=16] {'pz'}, dimensions={0} | all-to-all | bytes 4456448 | tf_op jit(solution)/shard_map/all_to_all | solution.py:287
  39.0 0.0 copy-done
  39.0 0.0 copy-done.1
  39.0 2.6 %y_transform.1 = f32[2,16,4,8,8,128]{5,4,3,2,1,0:T(8,128)S(1)} custom-call(f32[16,272,128]{2,1,0:T(8,128)S(1)} %all_to_all.10.data_ref, bf16[2,512,256]{2,1,0:T(8,128)(2,1)S(1)} %copy-done.1, bf16[2,512,256]{2,1,0:T(8,128)(2,1)S(1)} %copy-done), custom_call_target="tpu_custom_call" | custom-call | tf_op jit(solution)/shard_map/y_transform/pallas_call | solution.py:289
  41.7 0.0 copy-start.2
  41.7 0.0 copy-start.3
  41.7 108.2 %all_to_all.11 = f32[32,256,128]{2,1,0:T(8,128)S(1)} all-to-all(f32[32,256,128]{2,1,0:T(8,128)S(1)} %bitcast.2), channel_id=1, replica_groups={{0,16,32,48,64,80,96,112,128,144,160,176,192,208,224,240,15,31,47,63,79..., dimensions={0} | all-to-all | bytes 8388608 | tf_op jit(solution)/shard_map/all_to_all | solution.py:298
  149.9 0.0 copy-done.2
  149.9 0.0 copy-done.3
  149.9 3.9 %x_transform.1 = (f32[32,32,256]{2,1,0:T(8,128)}, f32[32,32,256]{2,1,0:T(8,128)}, f32[2,32,32,256]{3,2,1,0:T(8,128)}) custom-call(f32[2,16,256,128]{3,2,1,0:T(8,128)S(1)} %bitcast.3, bf16[256,256]{1,0:T(8,128)(2,1)S(1)} %copy-done.3, bf16[256,256]{1,0:T(8,128)(2,1)S(1)} %copy-done.2), custom_call_target="tpu_custom_call" | custom-call | tf_op jit(solution)/shard_map/x_transform/pallas_call | solution.py:306
Async XLA Ops:
  5.0 34.0 %copy-start = (bf16[2,512,256]{2,1,0:T(8,128)(2,1)S(1)}, bf16[2,512,256]{2,1,0:T(8,128)(2,1)}, u32[]{:S(2)}) copy-start(bf16[2,512,256]{2,1,0:T(8,128)(2,1)} %constant.15.clone.low_ref) | copy-start | bytes 1572868
  5.0 34.0 %copy-start.1 = (bf16[2,512,256]{2,1,0:T(8,128)(2,1)S(1)}, bf16[2,512,256]{2,1,0:T(8,128)(2,1)}, u32[]{:S(2)}) copy-start(bf16[2,512,256]{2,1,0:T(8,128)(2,1)} %constant.14.clone.high_ref) | copy-start | bytes 1572868
  41.7 108.2 %copy-start.2 = (bf16[256,256]{1,0:T(8,128)(2,1)S(1)}, bf16[256,256]{1,0:T(8,128)(2,1)}, u32[]{:S(2)}) copy-start(bf16[256,256]{1,0:T(8,128)(2,1)} %constant.17.clone.low_ref) | copy-start | bytes 393220
  41.7 108.2 %copy-start.3 = (bf16[256,256]{1,0:T(8,128)(2,1)S(1)}, bf16[256,256]{1,0:T(8,128)(2,1)}, u32[]{:S(2)}) copy-start(bf16[256,256]{1,0:T(8,128)(2,1)} %constant.16.clone.high_ref) | copy-start | bytes 393220
